TPU v7x, 512 devices: a whole 4x4x16 slice. The times are simulated.
512 devices in a mesh: gx: 16 (over y, z_hi), gy: 8 (over z_lo, core), gz: 4 (over x).
Axes of the slice: x: 4, y: 4, z: 16 (z_hi: 4, z_lo: 4; z = z_hi * 4 + z_lo), core: 2. Of those that a mesh axis runs over, the one named last changes fastest.
Arguments:
- e_field: float32 [3, 64, 128, 512], P(None, 'gx', 'gy', 'gz'), may hold values from -6 to 6
- h_field: float32 [3, 64, 128, 512], P(None, 'gx', 'gy', 'gz'), may hold values from -6 to 6
- current: float32 [3, 64, 128, 512], P(None, 'gx', 'gy', 'gz'), may hold values from -6 to 6
- material: int32 [64, 128, 512], P('gx', 'gy', 'gz'), may hold values from 0 to 2
- sigma_table: float32 [3], replicated, may hold values from 0.05 to 2
- gamma_table: float32 [3], replicated, may hold values from 0.05 to 1
- plasma_table: float32 [3], replicated, may hold values from 0.3 to 2
- g_kernel: float32 [4], replicated, may hold values from -4 to 4
- surf_cell: int32 [16, 8, 4, 1024], P('gx', 'gy', 'gz'), may hold values from 0 to 8191
- surf_owner: int32 [16, 8, 4, 1024, 1], P('gx', 'gy', 'gz'), may hold values from 0 to 127; in each aligned block of 1024 rows (0 to 1023, 1024 to 2047, ..., all dimensions but the last counted through in order) at most 12 rows name the same one
- surf_tile: int32 [16, 8, 4, 1024], P('gx', 'gy', 'gz'), may hold values from 0 to 127
- surf_normal: int32 [16, 8, 4, 1024], P('gx', 'gy', 'gz'), may hold values from 0 to 5
- row_count: int32 [16, 8, 4], P('gx', 'gy', 'gz'), may hold values from 256 to 1024, as said below
Outputs:
- e_out: float32 [3, 64, 128, 512], P(None, 'gx', 'gy', 'gz')
- h_out: float32 [3, 64, 128, 512], P(None, 'gx', 'gy', 'gz')
- force: float32 [3, 65536], P(None, ('gx', 'gy', 'gz'))
Inputs may be any that keep to these rules, and one draw needn't show every extreme that they name: `surf_owner`: among the slots of one device no owner is named more than 12 times, a bound that some block reaches. `row_count`: some brick has all 1024 slots live.
All inputs are finite; a program needn't handle non-finite values.
Results may differ from a plain program's by a relative error of at most 0.00019.
Values sent between devices are 32-bit elements; how exact they have to be, the bound alone decides.
A program may use at most 64 MiB of HBM per device.

v0:
```python
import jax
import jax.numpy as jnp
from jax import lax
from jax.sharding import PartitionSpec as P

TILE_DEV = 128


STEP_DT = 0.5
FACE_AREA = 0.25


def passed_along(shard, axis, by):
    peers = lax.axis_size(axis)
    pairs = [(i, i + by) for i in range(peers) if 0 <= i + by < peers]
    return lax.ppermute(shard, axis, pairs)


def lookup(material, table):
    result = jnp.zeros(material.shape, table.dtype)
    for which in range(table.shape[0]):
        result = result + jnp.where(material == which, table[which], jnp.zeros((), table.dtype))
    return result


def coefficients(material, sigma_table, gamma_table, plasma_table):
    sigma = lookup(material, sigma_table)
    gamma = lookup(material, gamma_table)
    plasma = lookup(material, plasma_table)
    keep_e = (1.0 - sigma * STEP_DT / 2) / (1.0 + sigma * STEP_DT / 2)
    gain_e = STEP_DT / (1.0 + sigma * STEP_DT / 2)
    keep_j = (1.0 - gamma * STEP_DT / 2) / (1.0 + gamma * STEP_DT / 2)
    gain_j = plasma * STEP_DT / (1.0 + gamma * STEP_DT / 2)
    return (keep_e, gain_e, keep_j, gain_j)


def row_forces(elec_rows, magn_rows, normal):
    axis_of = normal // 2
    sign_of = (1 - 2 * (normal % 2)).astype(elec_rows.dtype)
    picked = (axis_of[None, :] == jnp.arange(3, dtype=jnp.int32)[:, None]).astype(elec_rows.dtype)
    elec_n = jnp.sum(elec_rows * picked, axis=0)
    magn_n = jnp.sum(magn_rows * picked, axis=0)
    energy = 0.5 * (jnp.sum(elec_rows * elec_rows, axis=0) + jnp.sum(magn_rows * magn_rows, axis=0))
    return sign_of * (elec_rows * elec_n + magn_rows * magn_n - picked * energy)


def curl_upper(electric):
    rim_x = passed_along(electric[1:3, :1], "gx", -1)
    rim_y = passed_along(electric[0::2, :, :1], "gy", -1)
    rim_z = passed_along(electric[0:2, :, :, :1], "gz", -1)
    elec_x, elec_y, elec_z = (electric[0], electric[1], electric[2])
    y_next_x = jnp.concatenate([elec_y[1:], rim_x[0]], 0)
    z_next_x = jnp.concatenate([elec_z[1:], rim_x[1]], 0)
    x_next_y = jnp.concatenate([elec_x[:, 1:], rim_y[0]], 1)
    z_next_y = jnp.concatenate([elec_z[:, 1:], rim_y[1]], 1)
    x_next_z = jnp.concatenate([elec_x[:, :, 1:], rim_z[0]], 2)
    y_next_z = jnp.concatenate([elec_y[:, :, 1:], rim_z[1]], 2)
    curl_x = z_next_y - elec_z - (y_next_z - elec_y)
    curl_y = x_next_z - elec_x - (z_next_x - elec_z)
    curl_z = y_next_x - elec_y - (x_next_y - elec_x)
    return jnp.stack([curl_x, curl_y, curl_z])


def curl_lower(magnetic):
    rim_x = passed_along(magnetic[1:3, -1:], "gx", 1)
    rim_y = passed_along(magnetic[0::2, :, -1:], "gy", 1)
    rim_z = passed_along(magnetic[0:2, :, :, -1:], "gz", 1)
    magn_x, magn_y, magn_z = (magnetic[0], magnetic[1], magnetic[2])
    y_prev_x = jnp.concatenate([rim_x[0], magn_y[:-1]], 0)
    z_prev_x = jnp.concatenate([rim_x[1], magn_z[:-1]], 0)
    x_prev_y = jnp.concatenate([rim_y[0], magn_x[:, :-1]], 1)
    z_prev_y = jnp.concatenate([rim_y[1], magn_z[:, :-1]], 1)
    x_prev_z = jnp.concatenate([rim_z[0], magn_x[:, :, :-1]], 2)
    y_prev_z = jnp.concatenate([rim_z[1], magn_y[:, :, :-1]], 2)
    curl_x = magn_z - z_prev_y - (magn_y - y_prev_z)
    curl_y = magn_x - x_prev_z - (magn_z - z_prev_x)
    curl_z = magn_y - y_prev_x - (magn_x - x_prev_y)
    return jnp.stack([curl_x, curl_y, curl_z])


def local(
    e_field,
    h_field,
    current,
    material,
    sigma_table,
    gamma_table,
    plasma_table,
    g_kernel,
    surf_cell,
    surf_owner,
    surf_tile,
    surf_normal,
    row_count,
):
    keep_e, gain_e, keep_j, gain_j = coefficients(material, sigma_table, gamma_table, plasma_table)
    electric, magnetic, drude = (e_field, h_field, current)
    slot_cells = surf_cell.reshape(-1)
    normal = surf_normal.reshape(-1)
    owners = surf_owner.reshape(-1)
    tile_ids = surf_tile.reshape(-1)
    slot_total = slot_cells.shape[0]
    live_mask = (jnp.arange(slot_total, dtype=jnp.int32) < row_count.reshape(())).astype(
        jnp.float32
    )
    summed = jnp.zeros((3, slot_total), jnp.float32)
    for moment in range(g_kernel.shape[0]):
        magnetic = magnetic - STEP_DT * curl_upper(electric)
        curl_magn = curl_lower(magnetic)
        drude = keep_j * drude + gain_j * electric
        electric = keep_e * electric + gain_e * (curl_magn - drude)
        elec_rows = electric.reshape(3, -1)[:, slot_cells]
        magn_rows = magnetic.reshape(3, -1)[:, slot_cells]
        summed = summed + g_kernel[moment] * row_forces(elec_rows, magn_rows, normal)
    row_force = FACE_AREA * summed * live_mask
    groups = lax.axis_size("gx") * lax.axis_size("gy")
    capacity = 3 * slot_total // (2 * groups)
    owner_hot = (owners[:, None] == jnp.arange(groups, dtype=jnp.int32)[None, :]).astype(jnp.int32)
    ranks = jnp.sum(jnp.cumsum(owner_hot, axis=0) * owner_hot, axis=1) - 1
    force_buf = jnp.zeros((3, capacity, groups), jnp.float32).at[:, ranks, owners].set(row_force)
    tile_buf = (
        jnp.full((1, capacity, groups), -1.0, jnp.float32)
        .at[0, ranks, owners]
        .set(tile_ids.astype(jnp.float32))
    )
    got_force, got_tile = (
        lax.all_to_all(force_buf, ("gx", "gy"), split_axis=2, concat_axis=2, tiled=True),
        lax.all_to_all(tile_buf, ("gx", "gy"), split_axis=2, concat_axis=2, tiled=True),
    )
    tile_hot = (
        got_tile[0][:, :, None] == jnp.arange(TILE_DEV, dtype=jnp.float32)[None, None, :]
    ).astype(jnp.float32)
    force = jnp.einsum("acs,cst->at", got_force, tile_hot, precision=lax.Precision.HIGHEST)
    return (electric, magnetic, force)


def solution(mesh):
    return jax.shard_map(
        local,
        mesh=mesh,
        in_specs=(
            P(None, "gx", "gy", "gz"),
            P(None, "gx", "gy", "gz"),
            P(None, "gx", "gy", "gz"),
            P("gx", "gy", "gz"),
            P(),
            P(),
            P(),
            P(),
            P("gx", "gy", "gz", None),
            P("gx", "gy", "gz", None, None),
            P("gx", "gy", "gz", None),
            P("gx", "gy", "gz", None),
            P("gx", "gy", "gz"),
        ),
        out_specs=(
            P(None, "gx", "gy", "gz"),
            P(None, "gx", "gy", "gz"),
            P(None, ("gx", "gy", "gz")),
        ),
        check_vma=False,
    )
```

profile of v0, /device:TPU:1, one launch (start us, length us, event | category | flops | bytes accessed | tf_op | source)
XLA Modules:
  0.0 241.5 jit_solution(926793492307616486)
XLA Ops:
  1.5 8.8 %collective-permute-start = (f32[2,4,1,128]{3,2,1,0:T(1,128)S(1)}, f32[2,4,1,128]{3,2,1,0:T(1,128)S(1)}, u32[]{:S(2)}, u32[]{:S(2)}) collective-permute-start(f32[2,4,1,128]{3,2,1,0:T(1,128)S(1)} %slice.514), channel_id=1, source_target_pairs={{4,0},{8,4},{12,8},{16,12},{20,16},{24,20},{28,24},{5,1},{9,5},{13... | collective-permute-start | bytes 12296 | tf_op jit(solution)/shard_map/ppermute | solution.py:16
  19.6 4.3 %scatter_custom_fusion.1 = f32[1536]{0:T(1024)S(1)} fusion(s32[1024]{0:T(1024)S(1)} %broadcast_select_fusion, f32[1024]{0:T(1024)S(1)} %bitcast.301, f32[]{:T(128)} %constant.91.clone.1), kind=kCustom, calls=%fused_computation.263 | custom fusion | bytes 6148
  24.7 15.0 %all-to-all-start.1 = ((f32[1,12,128]{1,0,2:T(1,128)}), f32[1,12,128]{1,0,2:T(1,128)S(1)}, u32[]{:S(2)}, u32[]{:S(2)}) async-start(f32[1,12,128]{1,0,2:T(1,128)} %copy.102), calls=%async_computation.1 | async-start | bytes 131072 | tf_op jit(solution)/shard_map/all_to_all | solution.py:128
  51.2 5.8 %add_divide_fusion = (f32[4,16,128]{2,1,0:T(8,128)S(1)}, f32[4,16,128]{2,1,0:T(8,128)S(1)}, f32[4,16,128]{2,1,0:T(8,128)S(1)}) fusion(pred[4,16,128]{2,1,0:T(8,128)(4,1)S(1)} %get-tuple-element.38, pred[4,16,128]{2,1,0:T(8,128)(4,1)S(1)} %get-tuple-element.37, pred[4,16,128]{2,1,0:T(8,128)(4,1)S(1)} %get-tuple-element.36, f32[]{:T(128)} %bitcast.2, ...), kind=kLoop, calls=%fused_computation.155 | loop fusion | flops 196608 | bytes 122916 | tf_op jit(solution)/shard_map/div | solution.py:31
  57.4 3.5 %collective-permute-start.3 = (f32[2,4,1,128]{3,2,1,0:T(1,128)S(1)}, f32[2,4,1,128]{3,2,1,0:T(1,128)S(1)}, u32[]{:S(2)}, u32[]{:S(2)}) collective-permute-start(f32[2,4,1,128]{3,2,1,0:T(1,128)S(1)} %slice.531), channel_id=1, source_target_pairs={{0,4},{4,8},{8,12},{12,16},{16,20},{20,24},{24,28},{1,5},{5,9},{9,... | collective-permute-start | bytes 12296 | tf_op jit(solution)/shard_map/ppermute | solution.py:16
  61.0 7.0 %collective-permute-start.5 = (f32[2,1,16,128]{3,2,1,0:T(8,128)S(1)}, f32[2,1,16,128]{3,2,1,0:T(8,128)S(1)}, u32[]{:S(2)}, u32[]{:S(2)}) collective-permute-start(f32[2,1,16,128]{3,2,1,0:T(8,128)S(1)} %slice.704), channel_id=1, source_target_pairs={{0,32},{32,64},{64,96},{96,128},{128,160},{160,192},{192,224},{224... | collective-permute-start | bytes 49160 | tf_op jit(solution)/shard_map/ppermute | solution.py:16
  68.0 4.3 %collective-permute-start.4 = (f32[2,4,16,1]{3,2,1,0:T(8,128)S(1)}, f32[2,4,16,1]{3,2,1,0:T(8,128)S(1)}, u32[]{:S(2)}, u32[]{:S(2)}) collective-permute-start(f32[2,4,16,1]{3,2,1,0:T(8,128)S(1)} %slice.698), channel_id=1, source_target_pairs={{0,1},{1,2},{2,3},{4,5},{5,6},{6,7},{8,9},{9,10},{10,11},{12,13},{... | collective-permute-start | bytes 1544 | tf_op jit(solution)/shard_map/ppermute | solution.py:16
  74.9 5.0 %gather_fusion.1 = f32[1024,3]{1,0:T(8,128)S(1)} fusion(f32[3,8192]{0,1:T(8,128)} %bitcast.285, s32[1024]{0:T(1024)S(1)} %broadcast_clamp_fusion), kind=kCustom, calls=%fused_computation.1 | custom fusion | bytes 28672 | tf_op jit(solution)/shard_map/gather | solution.py:113
  85.1 2.6 %copy.83 = f32[3,4,16,128]{0,3,2,1:T(8,128)} copy(f32[3,4,16,128]{3,2,1,0:T(8,128)S(1)} %fusion.9) | data formatting | bytes 196608 | tf_op jit(solution)/shard_map/add | solution.py:111
  87.7 5.0 %gather_fusion = f32[1024,3]{1,0:T(8,128)S(1)} fusion(f32[3,8192]{0,1:T(8,128)} %bitcast.286, s32[1024]{0:T(1024)S(1)} %broadcast_clamp_fusion), kind=kCustom, calls=%fused_computation | custom fusion | bytes 28672 | tf_op jit(solution)/shard_map/gather | solution.py:112
  93.2 3.6 %collective-permute-start.9 = (f32[2,4,1,128]{3,2,1,0:T(1,128)S(1)}, f32[2,4,1,128]{3,2,1,0:T(1,128)S(1)}, u32[]{:S(2)}, u32[]{:S(2)}) collective-permute-start(f32[2,4,1,128]{3,2,1,0:T(1,128)S(1)} %slice.573), channel_id=1, source_target_pairs={{0,4},{4,8},{8,12},{12,16},{16,20},{20,24},{24,28},{1,5},{5,9},{9,... | collective-permute-start | bytes 12296 | tf_op jit(solution)/shard_map/ppermute | solution.py:16
  96.9 8.2 %collective-permute-start.11 = (f32[2,1,16,128]{3,2,1,0:T(8,128)S(1)}, f32[2,1,16,128]{3,2,1,0:T(8,128)S(1)}, u32[]{:S(2)}, u32[]{:S(2)}) collective-permute-start(f32[2,1,16,128]{3,2,1,0:T(8,128)S(1)} %slice.738), channel_id=1, source_target_pairs={{0,32},{32,64},{64,96},{96,128},{128,160},{160,192},{192,224},{224... | collective-permute-start | bytes 49160 | tf_op jit(solution)/shard_map/ppermute | solution.py:16
  105.1 4.3 %collective-permute-start.10 = (f32[2,4,16,1]{3,2,1,0:T(8,128)S(1)}, f32[2,4,16,1]{3,2,1,0:T(8,128)S(1)}, u32[]{:S(2)}, u32[]{:S(2)}) collective-permute-start(f32[2,4,16,1]{3,2,1,0:T(8,128)S(1)} %slice.732), channel_id=1, source_target_pairs={{0,1},{1,2},{2,3},{4,5},{5,6},{6,7},{8,9},{9,10},{10,11},{12,13},{... | collective-permute-start | bytes 1544 | tf_op jit(solution)/shard_map/ppermute | solution.py:16
  109.4 2.6 %copy.89 = f32[3,4,16,128]{0,3,2,1:T(8,128)} copy(f32[3,4,16,128]{3,2,1,0:T(8,128)S(1)} %fusion.10) | data formatting | bytes 196608 | tf_op jit(solution)/shard_map/sub | solution.py:108
  112.0 5.0 %gather_fusion.3 = f32[1024,3]{1,0:T(8,128)S(1)} fusion(f32[3,8192]{0,1:T(8,128)} %bitcast.287, s32[1024]{0:T(1024)S(1)} %broadcast_clamp_fusion), kind=kCustom, calls=%fused_computation.3 | custom fusion | bytes 28672 | tf_op jit(solution)/shard_map/gather | solution.py:113
  124.8 5.0 %gather_fusion.2 = f32[1024,3]{1,0:T(8,128)S(1)} fusion(f32[3,8192]{0,1:T(8,128)} %bitcast.288, s32[1024]{0:T(1024)S(1)} %broadcast_clamp_fusion), kind=kCustom, calls=%fused_computation.2 | custom fusion | bytes 28672 | tf_op jit(solution)/shard_map/gather | solution.py:112
  130.3 3.6 %collective-permute-start.15 = (f32[2,4,1,128]{3,2,1,0:T(1,128)S(1)}, f32[2,4,1,128]{3,2,1,0:T(1,128)S(1)}, u32[]{:S(2)}, u32[]{:S(2)}) collective-permute-start(f32[2,4,1,128]{3,2,1,0:T(1,128)S(1)} %slice.609), channel_id=1, source_target_pairs={{0,4},{4,8},{8,12},{12,16},{16,20},{20,24},{24,28},{1,5},{5,9},{9,... | collective-permute-start | bytes 12296 | tf_op jit(solution)/shard_map/ppermute | solution.py:16
  134.0 8.2 %collective-permute-start.17 = (f32[2,1,16,128]{3,2,1,0:T(8,128)S(1)}, f32[2,1,16,128]{3,2,1,0:T(8,128)S(1)}, u32[]{:S(2)}, u32[]{:S(2)}) collective-permute-start(f32[2,1,16,128]{3,2,1,0:T(8,128)S(1)} %slice.772), channel_id=1, source_target_pairs={{0,32},{32,64},{64,96},{96,128},{128,160},{160,192},{192,224},{224... | collective-permute-start | bytes 49160 | tf_op jit(solution)/shard_map/ppermute | solution.py:16
  142.1 4.3 %collective-permute-start.16 = (f32[2,4,16,1]{3,2,1,0:T(8,128)S(1)}, f32[2,4,16,1]{3,2,1,0:T(8,128)S(1)}, u32[]{:S(2)}, u32[]{:S(2)}) collective-permute-start(f32[2,4,16,1]{3,2,1,0:T(8,128)S(1)} %slice.766), channel_id=1, source_target_pairs={{0,1},{1,2},{2,3},{4,5},{5,6},{6,7},{8,9},{9,10},{10,11},{12,13},{... | collective-permute-start | bytes 1544 | tf_op jit(solution)/shard_map/ppermute | solution.py:16
  146.5 2.6 %copy.93 = f32[3,4,16,128]{0,3,2,1:T(8,128)} copy(f32[3,4,16,128]{3,2,1,0:T(8,128)S(1)} %fusion.13) | data formatting | bytes 196608 | tf_op jit(solution)/shard_map/sub | solution.py:108
  149.1 5.0 %gather_fusion.5 = f32[1024,3]{1,0:T(8,128)S(1)} fusion(f32[3,8192]{0,1:T(8,128)} %bitcast.289, s32[1024]{0:T(1024)S(1)} %broadcast_clamp_fusion), kind=kCustom, calls=%fused_computation.5 | custom fusion | bytes 28672 | tf_op jit(solution)/shard_map/gather | solution.py:113
  159.2 2.6 %copy.91 = f32[3,4,16,128]{0,3,2,1:T(8,128)} copy(f32[3,4,16,128]{3,2,1,0:T(8,128)S(1)} %fusion.15) | data formatting | bytes 196608 | tf_op jit(solution)/shard_map/add | solution.py:111
  161.9 5.0 %gather_fusion.4 = f32[1024,3]{1,0:T(8,128)S(1)} fusion(f32[3,8192]{0,1:T(8,128)} %bitcast.290, s32[1024]{0:T(1024)S(1)} %broadcast_clamp_fusion), kind=kCustom, calls=%fused_computation.4 | custom fusion | bytes 28672 | tf_op jit(solution)/shard_map/gather | solution.py:112
  167.4 3.6 %collective-permute-start.21 = (f32[2,4,1,128]{3,2,1,0:T(1,128)S(1)}, f32[2,4,1,128]{3,2,1,0:T(1,128)S(1)}, u32[]{:S(2)}, u32[]{:S(2)}) collective-permute-start(f32[2,4,1,128]{3,2,1,0:T(1,128)S(1)} %slice.645), channel_id=1, source_target_pairs={{0,4},{4,8},{8,12},{12,16},{16,20},{20,24},{24,28},{1,5},{5,9},{9,... | collective-permute-start | bytes 12296 | tf_op jit(solution)/shard_map/ppermute | solution.py:16
  171.1 8.2 %collective-permute-start.23 = (f32[2,1,16,128]{3,2,1,0:T(8,128)S(1)}, f32[2,1,16,128]{3,2,1,0:T(8,128)S(1)}, u32[]{:S(2)}, u32[]{:S(2)}) collective-permute-start(f32[2,1,16,128]{3,2,1,0:T(8,128)S(1)} %slice.806), channel_id=1, source_target_pairs={{0,32},{32,64},{64,96},{96,128},{128,160},{160,192},{192,224},{224... | collective-permute-start | bytes 49160 | tf_op jit(solution)/shard_map/ppermute | solution.py:16
  179.3 4.5 %collective-permute-start.22 = (f32[2,4,16,1]{3,2,1,0:T(8,128)S(1)}, f32[2,4,16,1]{3,2,1,0:T(8,128)S(1)}, u32[]{:S(2)}, u32[]{:S(2)}) collective-permute-start(f32[2,4,16,1]{3,2,1,0:T(8,128)S(1)} %slice.800), channel_id=1, source_target_pairs={{0,1},{1,2},{2,3},{4,5},{5,6},{6,7},{8,9},{9,10},{10,11},{12,13},{... | collective-permute-start | bytes 1544 | tf_op jit(solution)/shard_map/ppermute | solution.py:16
  183.7 2.6 %copy.97 = f32[3,4,16,128]{0,3,2,1:T(8,128)} copy(f32[3,4,16,128]{3,2,1,0:T(8,128)S(1)} %fusion.16) | data formatting | bytes 196608 | tf_op jit(solution)/shard_map/sub | solution.py:108
  186.4 5.0 %gather_fusion.7 = f32[1024,3]{1,0:T(8,128)S(1)} fusion(f32[3,8192]{0,1:T(8,128)} %bitcast.291, s32[1024]{0:T(1024)S(1)} %broadcast_clamp_fusion), kind=kCustom, calls=%fused_computation.7 | custom fusion | bytes 28672 | tf_op jit(solution)/shard_map/gather | solution.py:113
  194.4 5.0 %gather_fusion.6 = f32[1024,3]{1,0:T(8,128)S(1)} fusion(f32[3,8192]{0,1:T(8,128)} %bitcast.284, s32[1024]{0:T(1024)S(1)} %broadcast_clamp_fusion), kind=kCustom, calls=%fused_computation.6 | custom fusion | bytes 28672 | tf_op jit(solution)/shard_map/gather | solution.py:112
  202.5 3.3 %scatter_custom_fusion = f32[3,1536]{0,1:T(8,128)S(1)} fusion(s32[1024]{0:T(1024)S(1)} %broadcast_select_fusion.1, f32[1024,3]{1,0:T(8,128)S(1)} %copy.99, f32[]{:T(128)} %constant.82.clone.1), kind=kCustom, calls=%fused_computation.18 | custom fusion | bytes 18436
  207.4 10.4 %all-to-all-start = ((f32[3,12,128]{1,0,2:T(4,128)}), f32[3,12,128]{1,0,2:T(4,128)S(1)}, u32[]{:S(2)}, u32[]{:S(2)}) async-start(f32[3,12,128]{1,0,2:T(4,128)} %copy.101), calls=%async_computation | async-start | bytes 524288 | tf_op jit(solution)/shard_map/all_to_all | solution.py:127
  217.9 22.4 %all-to-all-done = f32[3,12,128]{1,0,2:T(4,128)S(1)} async-done(((f32[3,12,128]{1,0,2:T(4,128)}), f32[3,12,128]{1,0,2:T(4,128)S(1)}, u32[]{:S(2)}, u32[]{:S(2)}) %all-to-all-start) | async-done | bytes 18464 | tf_op jit(solution)/shard_map/all_to_all | solution.py:127
  (212 shorter events, 52.5 us)
Async XLA Ops:
  0.6 48.4 %copy-start.7 = (s32[2]{0:T(128)S(1)}, s32[2]{0:T(128)}, u32[]{:S(2)}) copy-start(s32[2]{0:T(128)} %constant.104) | copy-start | bytes 28
  0.6 48.4 %copy-start.6 = (s32[2]{0:T(128)S(1)}, s32[2]{0:T(128)}, u32[]{:S(2)}) copy-start(s32[2]{0:T(128)} %constant.101) | copy-start | bytes 28
  0.7 56.5 %copy-start = (f32[3,4,16,128]{3,2,1,0:T(8,128)S(1)}, f32[3,4,16,128]{3,2,1,0:T(8,128)}, u32[]{:S(2)}) copy-start(f32[3,4,16,128]{3,2,1,0:T(8,128)} %param.13) | copy-start | bytes 294916
  0.7 48.5 %copy-start.5 = (s32[4,16,128]{2,1,0:T(8,128)S(1)}, s32[4,16,128]{2,1,0:T(8,128)}, u32[]{:S(2)}) copy-start(s32[4,16,128]{2,1,0:T(8,128)} %param.16) | copy-start | bytes 98308
  0.7 56.5 %copy-start.2 = (f32[3,4,16,128]{3,2,1,0:T(8,128)S(1)}, f32[3,4,16,128]{3,2,1,0:T(8,128)}, u32[]{:S(2)}) copy-start(f32[3,4,16,128]{3,2,1,0:T(8,128)} %param.14) | copy-start | bytes 294916
  1.5 55.6 %collective-permute-start = (f32[2,4,1,128]{3,2,1,0:T(1,128)S(1)}, f32[2,4,1,128]{3,2,1,0:T(1,128)S(1)}, u32[]{:S(2)}, u32[]{:S(2)}) collective-permute-start(f32[2,4,1,128]{3,2,1,0:T(1,128)S(1)} %slice.514), channel_id=1, source_target_pairs={{4,0},{8,4},{12,8},{16,12},{20,16},{24,20},{28,24},{5,1},{9,5},{13... | collective-permute-start | bytes 12296 | tf_op jit(solution)/shard_map/ppermute | solution.py:16
  11.0 46.1 %collective-permute-start.2 = (f32[2,1,16,128]{3,2,1,0:T(8,128)S(1)}, f32[2,1,16,128]{3,2,1,0:T(8,128)S(1)}, u32[]{:S(2)}, u32[]{:S(2)}) collective-permute-start(f32[2,1,16,128]{3,2,1,0:T(8,128)S(1)} %slice.524), channel_id=1, source_target_pairs={{32,0},{64,32},{96,64},{128,96},{160,128},{192,160},{224,192},{256... | collective-permute-start | bytes 49160 | tf_op jit(solution)/shard_map/ppermute | solution.py:16
  13.1 43.9 %collective-permute-start.1 = (f32[2,4,16,1]{3,2,1,0:T(8,128)S(1)}, f32[2,4,16,1]{3,2,1,0:T(8,128)S(1)}, u32[]{:S(2)}, u32[]{:S(2)}) collective-permute-start(f32[2,4,16,1]{3,2,1,0:T(8,128)S(1)} %slice.518), channel_id=1, source_target_pairs={{1,0},{2,1},{3,2},{5,4},{6,5},{7,6},{9,8},{10,9},{11,10},{13,12},{... | collective-permute-start | bytes 1544 | tf_op jit(solution)/shard_map/ppermute | solution.py:16
  24.7 55.6 %copy-start.3 = (f32[3,4,16,128]{3,2,1,0:T(8,128)S(1)}, f32[3,4,16,128]{3,2,1,0:T(8,128)}, u32[]{:S(2)}) copy-start(f32[3,4,16,128]{3,2,1,0:T(8,128)} %param.15) | copy-start | bytes 294916
  24.7 182.7 %all-to-all-start.1 = ((f32[1,12,128]{1,0,2:T(1,128)}), f32[1,12,128]{1,0,2:T(1,128)S(1)}, u32[]{:S(2)}, u32[]{:S(2)}) async-start(f32[1,12,128]{1,0,2:T(1,128)} %copy.102), calls=%async_computation.1 | async-start | bytes 131072 | tf_op jit(solution)/shard_map/all_to_all | solution.py:128
  57.4 22.7 %collective-permute-start.3 = (f32[2,4,1,128]{3,2,1,0:T(1,128)S(1)}, f32[2,4,1,128]{3,2,1,0:T(1,128)S(1)}, u32[]{:S(2)}, u32[]{:S(2)}) collective-permute-start(f32[2,4,1,128]{3,2,1,0:T(1,128)S(1)} %slice.531), channel_id=1, source_target_pairs={{0,4},{4,8},{8,12},{12,16},{16,20},{20,24},{24,28},{1,5},{5,9},{9,... | collective-permute-start | bytes 12296 | tf_op jit(solution)/shard_map/ppermute | solution.py:16
  61.0 19.2 %collective-permute-start.5 = (f32[2,1,16,128]{3,2,1,0:T(8,128)S(1)}, f32[2,1,16,128]{3,2,1,0:T(8,128)S(1)}, u32[]{:S(2)}, u32[]{:S(2)}) collective-permute-start(f32[2,1,16,128]{3,2,1,0:T(8,128)S(1)} %slice.704), channel_id=1, source_target_pairs={{0,32},{32,64},{64,96},{96,128},{128,160},{160,192},{192,224},{224... | collective-permute-start | bytes 49160 | tf_op jit(solution)/shard_map/ppermute | solution.py:16
  68.0 12.1 %collective-permute-start.4 = (f32[2,4,16,1]{3,2,1,0:T(8,128)S(1)}, f32[2,4,16,1]{3,2,1,0:T(8,128)S(1)}, u32[]{:S(2)}, u32[]{:S(2)}) collective-permute-start(f32[2,4,16,1]{3,2,1,0:T(8,128)S(1)} %slice.698), channel_id=1, source_target_pairs={{0,1},{1,2},{2,3},{4,5},{5,6},{6,7},{8,9},{9,10},{10,11},{12,13},{... | collective-permute-start | bytes 1544 | tf_op jit(solution)/shard_map/ppermute | solution.py:16
  80.4 12.4 %collective-permute-start.6 = (f32[2,4,1,128]{3,2,1,0:T(1,128)S(1)}, f32[2,4,1,128]{3,2,1,0:T(1,128)S(1)}, u32[]{:S(2)}, u32[]{:S(2)}) collective-permute-start(f32[2,4,1,128]{3,2,1,0:T(1,128)S(1)} %slice.556), channel_id=1, source_target_pairs={{4,0},{8,4},{12,8},{16,12},{20,16},{24,20},{28,24},{5,1},{9,5},{13... | collective-permute-start | bytes 12296 | tf_op jit(solution)/shard_map/ppermute | solution.py:16
  82.4 10.5 %collective-permute-start.8 = (f32[2,1,16,128]{3,2,1,0:T(8,128)S(1)}, f32[2,1,16,128]{3,2,1,0:T(8,128)S(1)}, u32[]{:S(2)}, u32[]{:S(2)}) collective-permute-start(f32[2,1,16,128]{3,2,1,0:T(8,128)S(1)} %slice.722), channel_id=1, source_target_pairs={{32,0},{64,32},{96,64},{128,96},{160,128},{192,160},{224,192},{256... | collective-permute-start | bytes 49160 | tf_op jit(solution)/shard_map/ppermute | solution.py:16
  83.7 9.2 %collective-permute-start.7 = (f32[2,4,16,1]{3,2,1,0:T(8,128)S(1)}, f32[2,4,16,1]{3,2,1,0:T(8,128)S(1)}, u32[]{:S(2)}, u32[]{:S(2)}) collective-permute-start(f32[2,4,16,1]{3,2,1,0:T(8,128)S(1)} %slice.716), channel_id=1, source_target_pairs={{1,0},{2,1},{3,2},{5,4},{6,5},{7,6},{9,8},{10,9},{11,10},{13,12},{... | collective-permute-start | bytes 1544 | tf_op jit(solution)/shard_map/ppermute | solution.py:16
  93.2 24.0 %collective-permute-start.9 = (f32[2,4,1,128]{3,2,1,0:T(1,128)S(1)}, f32[2,4,1,128]{3,2,1,0:T(1,128)S(1)}, u32[]{:S(2)}, u32[]{:S(2)}) collective-permute-start(f32[2,4,1,128]{3,2,1,0:T(1,128)S(1)} %slice.573), channel_id=1, source_target_pairs={{0,4},{4,8},{8,12},{12,16},{16,20},{20,24},{24,28},{1,5},{5,9},{9,... | collective-permute-start | bytes 12296 | tf_op jit(solution)/shard_map/ppermute | solution.py:16
  96.9 20.3 %collective-permute-start.11 = (f32[2,1,16,128]{3,2,1,0:T(8,128)S(1)}, f32[2,1,16,128]{3,2,1,0:T(8,128)S(1)}, u32[]{:S(2)}, u32[]{:S(2)}) collective-permute-start(f32[2,1,16,128]{3,2,1,0:T(8,128)S(1)} %slice.738), channel_id=1, source_target_pairs={{0,32},{32,64},{64,96},{96,128},{128,160},{160,192},{192,224},{224... | collective-permute-start | bytes 49160 | tf_op jit(solution)/shard_map/ppermute | solution.py:16
  105.1 12.1 %collective-permute-start.10 = (f32[2,4,16,1]{3,2,1,0:T(8,128)S(1)}, f32[2,4,16,1]{3,2,1,0:T(8,128)S(1)}, u32[]{:S(2)}, u32[]{:S(2)}) collective-permute-start(f32[2,4,16,1]{3,2,1,0:T(8,128)S(1)} %slice.732), channel_id=1, source_target_pairs={{0,1},{1,2},{2,3},{4,5},{5,6},{6,7},{8,9},{9,10},{10,11},{12,13},{... | collective-permute-start | bytes 1544 | tf_op jit(solution)/shard_map/ppermute | solution.py:16
  117.5 12.4 %collective-permute-start.12 = (f32[2,4,1,128]{3,2,1,0:T(1,128)S(1)}, f32[2,4,1,128]{3,2,1,0:T(1,128)S(1)}, u32[]{:S(2)}, u32[]{:S(2)}) collective-permute-start(f32[2,4,1,128]{3,2,1,0:T(1,128)S(1)} %slice.592), channel_id=1, source_target_pairs={{4,0},{8,4},{12,8},{16,12},{20,16},{24,20},{28,24},{5,1},{9,5},{13... | collective-permute-start | bytes 12296 | tf_op jit(solution)/shard_map/ppermute | solution.py:16
  119.5 10.5 %collective-permute-start.14 = (f32[2,1,16,128]{3,2,1,0:T(8,128)S(1)}, f32[2,1,16,128]{3,2,1,0:T(8,128)S(1)}, u32[]{:S(2)}, u32[]{:S(2)}) collective-permute-start(f32[2,1,16,128]{3,2,1,0:T(8,128)S(1)} %slice.756), channel_id=1, source_target_pairs={{32,0},{64,32},{96,64},{128,96},{160,128},{192,160},{224,192},{256... | collective-permute-start | bytes 49160 | tf_op jit(solution)/shard_map/ppermute | solution.py:16
  120.8 9.2 %collective-permute-start.13 = (f32[2,4,16,1]{3,2,1,0:T(8,128)S(1)}, f32[2,4,16,1]{3,2,1,0:T(8,128)S(1)}, u32[]{:S(2)}, u32[]{:S(2)}) collective-permute-start(f32[2,4,16,1]{3,2,1,0:T(8,128)S(1)} %slice.750), channel_id=1, source_target_pairs={{1,0},{2,1},{3,2},{5,4},{6,5},{7,6},{9,8},{10,9},{11,10},{13,12},{... | collective-permute-start | bytes 1544 | tf_op jit(solution)/shard_map/ppermute | solution.py:16
  130.3 24.0 %collective-permute-start.15 = (f32[2,4,1,128]{3,2,1,0:T(1,128)S(1)}, f32[2,4,1,128]{3,2,1,0:T(1,128)S(1)}, u32[]{:S(2)}, u32[]{:S(2)}) collective-permute-start(f32[2,4,1,128]{3,2,1,0:T(1,128)S(1)} %slice.609), channel_id=1, source_target_pairs={{0,4},{4,8},{8,12},{12,16},{16,20},{20,24},{24,28},{1,5},{5,9},{9,... | collective-permute-start | bytes 12296 | tf_op jit(solution)/shard_map/ppermute | solution.py:16
  134.0 20.3 %collective-permute-start.17 = (f32[2,1,16,128]{3,2,1,0:T(8,128)S(1)}, f32[2,1,16,128]{3,2,1,0:T(8,128)S(1)}, u32[]{:S(2)}, u32[]{:S(2)}) collective-permute-start(f32[2,1,16,128]{3,2,1,0:T(8,128)S(1)} %slice.772), channel_id=1, source_target_pairs={{0,32},{32,64},{64,96},{96,128},{128,160},{160,192},{192,224},{224... | collective-permute-start | bytes 49160 | tf_op jit(solution)/shard_map/ppermute | solution.py:16
  142.1 12.1 %collective-permute-start.16 = (f32[2,4,16,1]{3,2,1,0:T(8,128)S(1)}, f32[2,4,16,1]{3,2,1,0:T(8,128)S(1)}, u32[]{:S(2)}, u32[]{:S(2)}) collective-permute-start(f32[2,4,16,1]{3,2,1,0:T(8,128)S(1)} %slice.766), channel_id=1, source_target_pairs={{0,1},{1,2},{2,3},{4,5},{5,6},{6,7},{8,9},{9,10},{10,11},{12,13},{... | collective-permute-start | bytes 1544 | tf_op jit(solution)/shard_map/ppermute | solution.py:16
  154.6 12.4 %collective-permute-start.18 = (f32[2,4,1,128]{3,2,1,0:T(1,128)S(1)}, f32[2,4,1,128]{3,2,1,0:T(1,128)S(1)}, u32[]{:S(2)}, u32[]{:S(2)}) collective-permute-start(f32[2,4,1,128]{3,2,1,0:T(1,128)S(1)} %slice.628), channel_id=1, source_target_pairs={{4,0},{8,4},{12,8},{16,12},{20,16},{24,20},{28,24},{5,1},{9,5},{13... | collective-permute-start | bytes 12296 | tf_op jit(solution)/shard_map/ppermute | solution.py:16
  156.5 10.5 %collective-permute-start.20 = (f32[2,1,16,128]{3,2,1,0:T(8,128)S(1)}, f32[2,1,16,128]{3,2,1,0:T(8,128)S(1)}, u32[]{:S(2)}, u32[]{:S(2)}) collective-permute-start(f32[2,1,16,128]{3,2,1,0:T(8,128)S(1)} %slice.790), channel_id=1, source_target_pairs={{32,0},{64,32},{96,64},{128,96},{160,128},{192,160},{224,192},{256... | collective-permute-start | bytes 49160 | tf_op jit(solution)/shard_map/ppermute | solution.py:16
  157.8 9.2 %collective-permute-start.19 = (f32[2,4,16,1]{3,2,1,0:T(8,128)S(1)}, f32[2,4,16,1]{3,2,1,0:T(8,128)S(1)}, u32[]{:S(2)}, u32[]{:S(2)}) collective-permute-start(f32[2,4,16,1]{3,2,1,0:T(8,128)S(1)} %slice.784), channel_id=1, source_target_pairs={{1,0},{2,1},{3,2},{5,4},{6,5},{7,6},{9,8},{10,9},{11,10},{13,12},{... | collective-permute-start | bytes 1544 | tf_op jit(solution)/shard_map/ppermute | solution.py:16
  167.4 24.1 %collective-permute-start.21 = (f32[2,4,1,128]{3,2,1,0:T(1,128)S(1)}, f32[2,4,1,128]{3,2,1,0:T(1,128)S(1)}, u32[]{:S(2)}, u32[]{:S(2)}) collective-permute-start(f32[2,4,1,128]{3,2,1,0:T(1,128)S(1)} %slice.645), channel_id=1, source_target_pairs={{0,4},{4,8},{8,12},{12,16},{16,20},{20,24},{24,28},{1,5},{5,9},{9,... | collective-permute-start | bytes 12296 | tf_op jit(solution)/shard_map/ppermute | solution.py:16
  171.1 20.5 %collective-permute-start.23 = (f32[2,1,16,128]{3,2,1,0:T(8,128)S(1)}, f32[2,1,16,128]{3,2,1,0:T(8,128)S(1)}, u32[]{:S(2)}, u32[]{:S(2)}) collective-permute-start(f32[2,1,16,128]{3,2,1,0:T(8,128)S(1)} %slice.806), channel_id=1, source_target_pairs={{0,32},{32,64},{64,96},{96,128},{128,160},{160,192},{192,224},{224... | collective-permute-start | bytes 49160 | tf_op jit(solution)/shard_map/ppermute | solution.py:16
  179.3 12.3 %collective-permute-start.22 = (f32[2,4,16,1]{3,2,1,0:T(8,128)S(1)}, f32[2,4,16,1]{3,2,1,0:T(8,128)S(1)}, u32[]{:S(2)}, u32[]{:S(2)}) collective-permute-start(f32[2,4,16,1]{3,2,1,0:T(8,128)S(1)} %slice.800), channel_id=1, source_target_pairs={{0,1},{1,2},{2,3},{4,5},{5,6},{6,7},{8,9},{9,10},{10,11},{12,13},{... | collective-permute-start | bytes 1544 | tf_op jit(solution)/shard_map/ppermute | solution.py:16
  207.4 32.9 %all-to-all-start = ((f32[3,12,128]{1,0,2:T(4,128)}), f32[3,12,128]{1,0,2:T(4,128)S(1)}, u32[]{:S(2)}, u32[]{:S(2)}) async-start(f32[3,12,128]{1,0,2:T(4,128)} %copy.101), calls=%async_computation | async-start | bytes 524288 | tf_op jit(solution)/shard_map/all_to_all | solution.py:127
  (2 other events, 42.8 us)
where the time goes:
time: 244 us; the launch traced here: 242 us
  starting transfers between devices  114 us (47%)
  local copies, waits for them, and re-layouts  84.5 us (35%)
  waiting for transfers between devices  22.5 us (9%)
  other arithmetic  17.3 us (7%)
  between operations  2.64 us (1%)
    ppermute x24, starting transfers between devices, passed_along(): return lax.ppermute(shard, axis, pairs)  88.1 us
    all_to_all x1, waiting for transfers between devices, local(): lax.all_to_all(force_buf, ('gx', 'gy'), split_axis=2, concat_axis=2, tile...  22.4 us
    gather x8, local copies, waits for them, and re-layouts, local(): elec_rows = electric.reshape(3, -1)[:, slot_cells]  20.7 us
    gather x8, local copies, waits for them, and re-layouts, local(): magn_rows = magnetic.reshape(3, -1)[:, slot_cells]  20.7 us
    all_to_all x1, starting transfers between devices, local(): lax.all_to_all(tile_buf, ('gx', 'gy'), split_axis=2, concat_axis=2, tiled...  15 us
    sub x4, local copies, waits for them, and re-layouts, local(): magnetic = magnetic - STEP_DT * curl_upper(electric)  10.5 us
    add x4, local copies, waits for them, and re-layouts, local(): electric = keep_e * electric + gain_e * (curl_magn - drude)  10.5 us
    all_to_all x1, starting transfers between devices, local(): lax.all_to_all(force_buf, ('gx', 'gy'), split_axis=2, concat_axis=2, tile...  10.4 us
  transfers between devices with their start and end apart: 26, of which 1 were waited for; matrix products, arithmetic and copies ran while one was open for 42% of the time, Pallas kernels for 0%

commit v1 on v0

v1 whole, which is shorter than its diff:
```python
import functools

import jax
import jax.numpy as jnp
from jax import lax
from jax.experimental import pallas as pl
from jax.experimental.pallas import tpu as pltpu
from jax.sharding import PartitionSpec as P

MESH = pl.DeviceIdType.MESH
F32 = jnp.float32
BF16 = jnp.bfloat16

DT = 0.5
FACE_AREA = 0.25
STEPS = 4
CX, CY, CZ = 4, 16, 128
SLOTS = 1024
TILE_DEV = 128
NGX, NGY, NGZ = 16, 8, 4
LANES = 16 * NGX

(XE, XQ, YE, YQ, ZE, ZQ, E_XZ, E_XY, E_YZ, E_YX, E_ZY, E_ZX) = range(12)
ROUTES = (
    (-1, 0, 0),
    (1, 0, 0),
    (0, -1, 0),
    (0, 1, 0),
    (0, 0, -1),
    (0, 0, 1),
    (1, 0, -1),
    (1, -1, 0),
    (0, 1, -1),
    (-1, 1, 0),
    (0, -1, 1),
    (-1, 0, 1),
)


def iota(shape, axis):
    return lax.broadcasted_iota(jnp.int32, shape, axis)


def dot(a, b, contract):
    return lax.dot_general(a, b, ((contract[:1], contract[1:]), ((), ())), preferred_element_type=F32)


def halves(x):
    high = x.astype(BF16)
    return high, (x - high.astype(F32)).astype(BF16)


def kernel(
    e_in,
    h_in,
    j_in,
    mat_in,
    cell_ref,
    owner_ref,
    tile_ref,
    normal_ref,
    sig_ref,
    gam_ref,
    pla_ref,
    g_ref,
    count_ref,
    e_out,
    h_out,
    force_ref,
    e_ref,
    h_ref,
    j_ref,
    part,
    mat_ref,
    coef,
    tensor,
    sx,
    rx,
    sy,
    ry,
    sz,
    rz,
    sr,
    rr,
    bucket,
    lane_hot,
    tile_hot,
    stl,
    rtl,
    sval,
    rval,
    sdense,
    rdense,
    in_sem,
    out_sem,
    hs_sem,
    hr_sem,
    ts_sem,
    tr_sem,
    vs_sem,
    vr_sem,
    ds_sem,
    dr_sem,
):
    gx, gy, gz = lax.axis_index("gx"), lax.axis_index("gy"), lax.axis_index("gz")

    loads = [
        pltpu.make_async_copy(src, dst, in_sem.at[n])
        for n, (src, dst) in enumerate(((e_in, e_ref), (h_in, h_ref), (j_in, j_ref), (mat_in, mat_ref)))
    ]
    for load in loads:
        load.start()

    def at(dx, dy, dz):
        where = {}
        if dx:
            where["gx"] = lax.rem(gx + (dx + NGX), NGX)
        if dy:
            where["gy"] = lax.rem(gy + (dy + NGY), NGY)
        if dz:
            where["gz"] = lax.rem(gz + (dz + NGZ), NGZ)
        return where

    barrier = pltpu.get_barrier_semaphore()
    greeted = list(ROUTES)
    greeted += [(0, d, 0) for d in range(2, NGY - 1)]
    greeted += [(d, 0, 0) for d in range(2, NGX - 1)]
    for route in greeted:
        pl.semaphore_signal(barrier, inc=1, device_id=at(*route), device_id_type=MESH)

    one, zero = jnp.float32(1.0), jnp.float32(0.0)
    low_x = jnp.where(gx > 0, one, zero)
    low_y = jnp.where(gy > 0, one, zero)
    low_z = jnp.where(gz > 0, one, zero)
    top_x = jnp.where(gx < NGX - 1, one, zero)
    top_y = jnp.where(gy < NGY - 1, one, zero)
    top_z = jnp.where(gz < NGZ - 1, one, zero)

    brick = (CX, CY, CZ)
    jj, kk = iota(brick, 1), iota(brick, 2)
    n_hot = (iota((16, 8, CZ), 0) == iota((16, 8, CZ), 2)).astype(F32)
    row_hot = (iota((CY, CZ), 0) == iota((CY, CZ), 1)).astype(F32)

    def y_next(f):
        return pltpu.roll(f, CY - 1, 1)

    def z_next(f):
        return pltpu.roll(f, CZ - 1, 2)

    def packed(columns):
        return jnp.sum(columns.reshape(16, 8, -1) * n_hot, axis=0)

    def unpacked(tile):
        return jnp.sum(tile[None] * n_hot, axis=2, keepdims=True).reshape(2, CX, CY, 1)

    def message(step, which):
        src, dst = {
            XE: (sx.at[step, 0], rx.at[step, 0]),
            XQ: (sx.at[step, 1], rx.at[step, 1]),
            YE: (sy.at[step, pl.ds(0, 2)], ry.at[step, pl.ds(0, 2)]),
            YQ: (sy.at[step, pl.ds(2, 2)], ry.at[step, pl.ds(2, 2)]),
            ZE: (sz.at[step, 0], rz.at[step, 0]),
            ZQ: (sz.at[step, 1], rz.at[step, 1]),
            E_XZ: (sr.at[step, 0], rr.at[step, 0]),
            E_XY: (sr.at[step, 1], rr.at[step, 1]),
            E_YX: (sr.at[step, 2], rr.at[step, 2]),
            E_ZX: (sr.at[step, 3], rr.at[step, 3]),
            E_YZ: (sy.at[step, 4], ry.at[step, 4]),
            E_ZY: (sy.at[step, 5], ry.at[step, 5]),
        }[which]
        return pltpu.make_async_remote_copy(
            src_ref=src,
            dst_ref=dst,
            send_sem=hs_sem.at[step, which],
            recv_sem=hr_sem.at[step, which],
            device_id=at(*ROUTES[which]),
            device_id_type=MESH,
        )

    def send_electric(step):
        ex, ey, ez = e_ref[0], e_ref[1], e_ref[2]
        sx[step, 0, 0] = ey[0]
        sx[step, 0, 1] = ez[0]
        message(step, XE).start()
        sr[step, 1] = ex[CX - 1, 0:1, :]
        sr[step, 2] = ey[0, CY - 1 : CY, :]
        sr[step, 0] = jnp.sum(ex[CX - 1, :, 0:1] * row_hot, axis=0, keepdims=True)
        sr[step, 3] = jnp.sum(ez[0, :, CZ - 1 : CZ] * row_hot, axis=0, keepdims=True)
        for which in (E_XY, E_YX, E_XZ, E_ZX):
            message(step, which).start()
        sy[step, 0] = ex[:, 0:1, :]
        sy[step, 1] = ez[:, 0:1, :]
        sy[step, 4] = ey[:, CY - 1 : CY, :]
        sy[step, 5] = ez[:, 0:1, :]
        sz[step, 0] = packed(e_ref[0:2][:, :, :, 0:1])
        for which in (YE, ZE, E_YZ, E_ZY):
            message(step, which).start()

    def send_magnetic(step):
        ex, ey, ez = e_ref[0], e_ref[1], e_ref[2]
        nothing = jnp.zeros((1, CY, CZ), F32)
        last_y, last_z = jj == CY - 1, kk == CZ - 1
        y_ez = jnp.where(last_y, zero, y_next(ez))
        y_ex = jnp.where(last_y, zero, y_next(ex))
        z_ey = jnp.where(last_z, zero, z_next(ey))
        z_ex = jnp.where(last_z, zero, z_next(ex))
        x_ez = jnp.concatenate([ez[1:], nothing], 0)
        x_ey = jnp.concatenate([ey[1:], nothing], 0)
        hx = h_ref[0] - DT * ((y_ez - ez) - (z_ey - ey))
        hy = h_ref[1] - DT * ((z_ex - ex) - (x_ez - ez))
        hz = h_ref[2] - DT * ((x_ey - ey) - (y_ex - ex))
        sx[step, 1, 0] = hy[CX - 1]
        sx[step, 1, 1] = hz[CX - 1]
        message(step, XQ).start()
        part[0], part[1], part[2] = hx, hy, hz
        sy[step, 2] = hx[:, CY - 1 : CY, :]
        sy[step, 3] = hz[:, CY - 1 : CY, :]
        sz[step, 1] = packed(part[0:2][:, :, :, CZ - 1 : CZ])
        message(step, YQ).start()
        message(step, ZQ).start()
        j_ref[...] = coef[2][None] * j_ref[...] + coef[3][None] * e_ref[...]

    def update(step):
        ex, ey, ez = e_ref[0], e_ref[1], e_ref[2]
        for which in range(12):
            message(step, which).wait_recv()
        above_x = rx[step, 0] * top_x
        above_y = ry[step, 0:2] * top_y
        above_z = unpacked(rz[step, 0]) * top_z
        hx, hy, hz = part[0], part[1], part[2]
        last_y, last_z = jj == CY - 1, kk == CZ - 1
        hx = hx + jnp.where(last_z, DT * above_z[1], zero) - jnp.where(last_y, DT * above_y[1], zero)
        hy = hy - jnp.where(last_z, DT * above_z[0], zero)
        hz = hz + jnp.where(last_y, DT * above_y[0], zero)
        hy = jnp.concatenate([hy[: CX - 1], (hy[CX - 1] + DT * above_x[1])[None]], 0)
        hz = jnp.concatenate([hz[: CX - 1], (hz[CX - 1] - DT * above_x[0])[None]], 0)
        h_ref[0], h_ref[1], h_ref[2] = hx, hy, hz
        e_xz = jnp.sum(rr[step, 0] * row_hot, axis=1, keepdims=True) * top_z
        e_zx = jnp.sum(rr[step, 3] * row_hot, axis=1, keepdims=True) * top_x
        e_xy = rr[step, 1] * top_y
        e_yx = rr[step, 2] * top_x
        e_yz = ry[step, 4] * top_z
        e_zy = ry[step, 5] * top_y
        jr, kr = iota((CY, CZ), 0), iota((CY, CZ), 1)
        below_xy = rx[step, 1, 0] + DT * ez[0] - jnp.where(kr == CZ - 1, DT * e_xz, zero)
        below_xz = rx[step, 1, 1] - DT * ey[0] + jnp.where(jr == CY - 1, DT * e_xy, zero)
        ky = iota((CX, 1, CZ), 2)
        below_yx = ry[step, 2] - DT * ez[:, 0:1, :] + jnp.where(ky == CZ - 1, DT * e_yz[:, :, 0:1], zero)
        below_yz = ry[step, 3] + DT * ex[:, 0:1, :]
        below_yz = jnp.concatenate([below_yz[: CX - 1], (below_yz[CX - 1] - DT * e_yx)[None]], 0)
        below_z = unpacked(rz[step, 1])
        jz = iota((CX, CY, 1), 1)
        below_zx = below_z[0] + DT * ey[:, :, 0:1] - jnp.where(jz == CY - 1, DT * e_zy[:, :, CZ - 1 : CZ], zero)
        below_zy = below_z[1] - DT * ex[:, :, 0:1]
        below_zy = jnp.concatenate([below_zy[: CX - 1], (below_zy[CX - 1] + DT * e_zx)[None]], 0)

        first_y, first_z = jj == 0, kk == 0
        y_hx = jnp.where(first_y, low_y * below_yx, pltpu.roll(hx, 1, 1))
        y_hz = jnp.where(first_y, low_y * below_yz, pltpu.roll(hz, 1, 1))
        z_hx = jnp.where(first_z, low_z * below_zx, pltpu.roll(hx, 1, 2))
        z_hy = jnp.where(first_z, low_z * below_zy, pltpu.roll(hy, 1, 2))
        x_hy = jnp.concatenate([(low_x * below_xy)[None], hy[: CX - 1]], 0)
        x_hz = jnp.concatenate([(low_x * below_xz)[None], hz[: CX - 1]], 0)
        keep, gain = coef[0], coef[1]
        e_ref[0] = keep * ex + gain * (((hz - y_hz) - (hy - z_hy)) - j_ref[0])
        e_ref[1] = keep * ey + gain * (((hx - z_hx) - (hz - x_hz)) - j_ref[1])
        e_ref[2] = keep * ez + gain * (((hy - x_hy) - (hx - y_hx)) - j_ref[2])

    def stress(step):
        ex, ey, ez = e_ref[0], e_ref[1], e_ref[2]
        hx, hy, hz = h_ref[0], h_ref[1], h_ref[2]
        g = g_ref[step]
        xx, yy, zz = ex * ex + hx * hx, ey * ey + hy * hy, ez * ez + hz * hz
        energy = 0.5 * (xx + yy + zz)
        found = (xx - energy, ex * ey + hx * hy, ex * ez + hx * hz, yy - energy, ey * ez + hy * hz, zz - energy)
        for n, value in enumerate(found):
            tensor[n] = g * value if step == 0 else tensor[n] + g * value

    def ranks_and_buckets():
        owner = owner_ref[...]
        block = SLOTS // 4
        groups = NGX * NGY
        earlier = (iota((block, block), 0) < iota((block, block), 1)).astype(F32).astype(BF16)
        lane = iota((1, block), 1)
        before = jnp.zeros((groups, 1), F32)
        made = jnp.zeros((5 * NGY, LANES), F32)
        for b in range(4):
            cut = slice(b * block, (b + 1) * block)
            own = owner[:, cut]
            hot = (own == iota((groups, block), 0)).astype(F32)
            ahead = dot(hot.astype(BF16), earlier, (1, 0)) + before
            rank = jnp.sum(ahead * hot, axis=0, keepdims=True).astype(jnp.int32)
            before = before + jnp.sum(hot, axis=1, keepdims=True)
            place = rank * NGX + lax.shift_right_logical(own, 3)
            place_hot = (place == iota((LANES, block), 0)).astype(F32).astype(BF16)
            cell, normal = cell_ref[:, cut], normal_ref[:, cut]
            live = (lane + b * block < count_ref[0]).astype(F32)
            weight = live * (FACE_AREA * (1 - 2 * (normal & 1)).astype(F32))
            mine = (own & 7) == iota((NGY, block), 0)
            entries = (
                (cell & 127).astype(F32),
                lax.shift_right_logical(cell, 7).astype(F32),
                weight,
                lax.shift_right_logical(normal, 1).astype(F32),
                tile_ref[:, cut].astype(F32),
            )
            rows = jnp.concatenate([jnp.where(mine, entry, zero) for entry in entries], 0)
            made = made + dot(rows.astype(BF16), place_hot, (1, 1))
        for n in range(5):
            bucket[n] = made[n * NGY : (n + 1) * NGY].reshape(NGY, 1, LANES)
        stl[...] = bucket[4]

    def to_gy(src, dst, send, recv, d):
        return pltpu.make_async_remote_copy(
            src_ref=src.at[lax.rem(gy + d, NGY)],
            dst_ref=dst.at[gy],
            send_sem=send.at[d],
            recv_sem=recv.at[d],
            device_id={"gy": lax.rem(gy + d, NGY)},
            device_id_type=MESH,
        )

    def from_gy(src, dst, send, recv, d):
        return pltpu.make_async_remote_copy(
            src_ref=src.at[lax.rem(gy + d, NGY)],
            dst_ref=dst.at[lax.rem(gy + NGY - d, NGY)],
            send_sem=send.at[d],
            recv_sem=recv.at[d],
            device_id={"gy": lax.rem(gy + d, NGY)},
            device_id_type=MESH,
        )

    def lane_hots():
        for n in range(NGY):
            lane_hot[n] = (bucket[0, n] == iota((CZ, LANES), 0).astype(F32)).astype(F32).astype(BF16)

    def tile_hots():
        for d in range(1, NGY):
            from_gy(stl, rtl, ts_sem, tr_sem, d).wait_recv()
        for n in range(NGY):
            tile_hot[n] = (rtl[n] == iota((TILE_DEV, LANES), 0).astype(F32)).astype(F32).astype(BF16)

    for load in loads:
        load.wait()
    material = mat_ref[...]

    def of_material(table):
        result = jnp.where(material == 0, table[0], zero)
        for which in (1, 2):
            result = jnp.where(material == which, table[which], result)
        return result

    sigma, gamma, plasma = of_material(sig_ref), of_material(gam_ref), of_material(pla_ref)
    coef[0] = (1.0 - sigma * DT / 2) / (1.0 + sigma * DT / 2)
    coef[1] = DT / (1.0 + sigma * DT / 2)
    coef[2] = (1.0 - gamma * DT / 2) / (1.0 + gamma * DT / 2)
    coef[3] = plasma * DT / (1.0 + gamma * DT / 2)

    pl.semaphore_wait(barrier, len(greeted))

    for step in range(STEPS):
        send_electric(step)
        send_magnetic(step)
        if step == 0:
            ranks_and_buckets()
            for d in range(1, NGY):
                to_gy(stl, rtl, ts_sem, tr_sem, d).start()
            rtl[gy] = stl[gy]
        else:
            stress(step - 1)
        if step == 1:
            lane_hots()
        if step == 2:
            tile_hots()
        update(step)
    stores = [
        pltpu.make_async_copy(src, dst, out_sem.at[n]) for n, (src, dst) in enumerate(((e_ref, e_out), (h_ref, h_out)))
    ]
    for store in stores:
        store.start()
    stress(STEPS - 1)

    cells = CX * CY
    high, low = halves(tensor[...].reshape(6 * cells, CZ))
    parts = jnp.concatenate([high, low], 1)
    for n in range(NGY):
        hot = lane_hot[n]
        read = dot(parts, jnp.concatenate([hot, hot], 0), (1, 0))
        row = bucket[1, n] == iota((cells, LANES), 0).astype(F32)
        xx, xy, xz, yy, yz, zz = [
            jnp.sum(jnp.where(row, read[c * cells : (c + 1) * cells], zero), axis=0, keepdims=True) for c in range(6)
        ]
        axis, weight = bucket[3, n], bucket[2, n]
        along_x, along_y = axis == 0.0, axis == 1.0
        sval[n, 0:1] = weight * jnp.where(along_x, xx, jnp.where(along_y, xy, xz))
        sval[n, 1:2] = weight * jnp.where(along_x, xy, jnp.where(along_y, yy, yz))
        sval[n, 2:3] = weight * jnp.where(along_x, xz, jnp.where(along_y, yz, zz))
    for d in range(1, NGY):
        to_gy(sval, rval, vs_sem, vr_sem, d).start()
    rval[gy] = sval[gy]

    for d in range(1, NGY):
        from_gy(sval, rval, vs_sem, vr_sem, d).wait_recv()
    row16 = iota((NGX * 16, LANES), 0)
    mine = (lax.shift_right_logical(row16, 4) == (iota((NGX * 16, LANES), 1) & (NGX - 1))).astype(F32).astype(BF16)
    dense = jnp.zeros((NGX * 16, TILE_DEV), F32)
    for n in range(NGY):
        value = jnp.concatenate([rval[n], jnp.zeros((5, LANES), F32)], 0)
        high = value.astype(BF16).astype(F32)
        both = jnp.concatenate([high, value - high], 0).astype(BF16)
        spread = jnp.concatenate([both] * NGX, 0) * mine
        dense = dense + dot(spread, tile_hot[n], (1, 1))
    dense = dense.reshape(NGX, 16, TILE_DEV)
    sdense[...] = (dense[:, 0:8] + dense[:, 8:16])[:, 0:3]

    def to_gx(d):
        return pltpu.make_async_remote_copy(
            src_ref=sdense.at[lax.rem(gx + d, NGX)],
            dst_ref=rdense.at[gx],
            send_sem=ds_sem.at[d],
            recv_sem=dr_sem.at[d],
            device_id={"gx": lax.rem(gx + d, NGX)},
            device_id_type=MESH,
        )

    for d in range(1, NGX):
        to_gx(d).start()
    rdense[gx] = sdense[gx]
    for d in range(1, NGX):
        pltpu.make_async_remote_copy(
            src_ref=sdense.at[lax.rem(gx + d, NGX)],
            dst_ref=rdense.at[lax.rem(gx + NGX - d, NGX)],
            send_sem=ds_sem.at[d],
            recv_sem=dr_sem.at[d],
            device_id={"gx": lax.rem(gx + d, NGX)},
            device_id_type=MESH,
        ).wait_recv()
    force_ref[...] = jnp.sum(rdense[...], axis=0)

    for step in range(STEPS):
        for which in range(12):
            message(step, which).wait_send()
    for d in range(1, NGY):
        to_gy(stl, rtl, ts_sem, tr_sem, d).wait_send()
        to_gy(sval, rval, vs_sem, vr_sem, d).wait_send()
    for d in range(1, NGX):
        to_gx(d).wait_send()
    for store in stores:
        store.wait()


def local(
    e_field,
    h_field,
    current,
    material,
    sigma_table,
    gamma_table,
    plasma_table,
    g_kernel,
    surf_cell,
    surf_owner,
    surf_tile,
    surf_normal,
    row_count,
):
    field = jax.ShapeDtypeStruct((3, CX, CY, CZ), F32)
    hbm = pl.BlockSpec(memory_space=pl.ANY)
    vmem = pl.BlockSpec(memory_space=pltpu.VMEM)
    smem = pl.BlockSpec(memory_space=pltpu.SMEM)
    dma = pltpu.SemaphoreType.DMA
    slots = [a.reshape(1, SLOTS) for a in (surf_cell, surf_owner, surf_tile, surf_normal)]
    return pl.pallas_call(
        kernel,
        out_shape=(field, field, jax.ShapeDtypeStruct((3, TILE_DEV), F32)),
        in_specs=[hbm] * 4 + [vmem] * 4 + [smem] * 5,
        out_specs=(hbm, hbm, vmem),
        scratch_shapes=[
            pltpu.VMEM((3, CX, CY, CZ), F32),
            pltpu.VMEM((3, CX, CY, CZ), F32),
            pltpu.VMEM((3, CX, CY, CZ), F32),
            pltpu.VMEM((3, CX, CY, CZ), F32),
            pltpu.VMEM((CX, CY, CZ), jnp.int32),
            pltpu.VMEM((4, CX, CY, CZ), F32),
            pltpu.VMEM((6, CX, CY, CZ), F32),
            pltpu.VMEM((STEPS, 2, 2, CY, CZ), F32),
            pltpu.VMEM((STEPS, 2, 2, CY, CZ), F32),
            pltpu.VMEM((STEPS, 6, CX, 1, CZ), F32),
            pltpu.VMEM((STEPS, 6, CX, 1, CZ), F32),
            pltpu.VMEM((STEPS, 2, 8, CZ), F32),
            pltpu.VMEM((STEPS, 2, 8, CZ), F32),
            pltpu.VMEM((STEPS, 4, 1, CZ), F32),
            pltpu.VMEM((STEPS, 4, 1, CZ), F32),
            pltpu.VMEM((5, NGY, 1, LANES), F32),
            pltpu.VMEM((NGY, CZ, LANES), BF16),
            pltpu.VMEM((NGY, TILE_DEV, LANES), BF16),
            pltpu.VMEM((NGY, 1, LANES), F32),
            pltpu.VMEM((NGY, 1, LANES), F32),
            pltpu.VMEM((NGY, 3, LANES), F32),
            pltpu.VMEM((NGY, 3, LANES), F32),
            pltpu.VMEM((NGX, 3, TILE_DEV), F32),
            pltpu.VMEM((NGX, 3, TILE_DEV), F32),
            dma((4,)),
            dma((2,)),
            dma((STEPS, 12)),
            dma((STEPS, 12)),
            dma((NGY,)),
            dma((NGY,)),
            dma((NGY,)),
            dma((NGY,)),
            dma((NGX,)),
            dma((NGX,)),
        ],
        compiler_params=pltpu.CompilerParams(
            collective_id=0, has_side_effects=True, vmem_limit_bytes=24 * 2**20
        ),
    )(
        e_field,
        h_field,
        current,
        material,
        *slots,
        sigma_table,
        gamma_table,
        plasma_table,
        g_kernel,
        row_count.reshape(1),
    )


def solution(mesh):
    cells = P("gx", "gy", "gz")
    field = P(None, "gx", "gy", "gz")
    slots = P("gx", "gy", "gz", None)
    return jax.shard_map(
        local,
        mesh=mesh,
        in_specs=(
            field,
            field,
            field,
            cells,
            P(),
            P(),
            P(),
            P(),
            slots,
            P("gx", "gy", "gz", None, None),
            slots,
            slots,
            cells,
        ),
        out_specs=(field, field, P(None, ("gx", "gy", "gz"))),
        check_vma=False,
    )
```

time: 244 us -> 69.8 us (0.29)
  starting transfers between devices: 114 us -> 0 us
  local copies, waits for them, and re-layouts: 84.5 us -> 7.33 us
  Pallas kernels: 0 us -> 60.7 us
  waiting for transfers between devices: 22.5 us -> 0 us
  other arithmetic: 17.3 us -> 0 us
    ppermute x24 -> x0, starting transfers between devices: 88.1 us -> none  [passed_along(): return lax.ppermute(shard, axis, pairs)]
    pallas_call x0 -> x1, Pallas kernels: none -> 60.7 us  [local(): pl.pallas_call(kernel, out_shape=(field, field, jax.ShapeDtypeStruct((3,...]
    gather x16 -> x0, local copies, waits for them, and re-layouts: 41.4 us -> none  [the longest x8 20.7 us: local(): elec_rows = electric.reshape(3, -1)[:, slot_cells]]
    all_to_all x2 -> x0, starting transfers between devices: 25.4 us -> none  [the longest x1 15 us: local(): lax.all_to_all(tile_buf, ('gx', 'gy'), split_axis=2, concat_axis=2, tiled...]
    all_to_all x2 -> x0, waiting for transfers between devices: 22.4 us -> none  [the longest x1 22.4 us: local(): lax.all_to_all(force_buf, ('gx', 'gy'), split_axis=2, concat_axis=2, tile...]
    add x4 -> x0, local copies, waits for them, and re-layouts: 10.5 us -> none  [local(): electric = keep_e * electric + gain_e * (curl_magn - drude)]
    sub x4 -> x0, local copies, waits for them, and re-layouts: 10.5 us -> none  [local(): magnetic = magnetic - STEP_DT * curl_upper(electric)]
    slice x60 -> x0, local copies, waits for them, and re-layouts: 9.33 us -> none  [the longest x3 4.15 us: lookup(): table[which]]
  transfers between devices with their start and end apart: 26 -> 0, of which waited for: 1 -> 0; matrix products, arithmetic and copies ran while one was open for 42% -> 0% of each run, Pallas kernels for 0% -> 0%
where the time goes in v1:
time: 69.8 us; the launch traced here: 69.4 us
  Pallas kernels  60.7 us (87%)
  local copies, waits for them, and re-layouts  7.33 us (11%)
  between operations  1.38 us (2%)
    pallas_call x1, Pallas kernels, local(): pl.pallas_call(kernel, out_shape=(field, field, jax.ShapeDtypeStruct((3,...  60.7 us
    unnamed x27, local copies, waits for them, and re-layouts  7.33 us

profile of v1, /device:TPU:1, one launch (start us, length us, event | category | flops | bytes accessed | tf_op | source)
XLA Modules:
  0.0 69.4 jit_solution(11595399302224514697)
XLA Ops:
  0.6 0.0 copy-start.10
  0.6 0.0 copy-start.11
  1.3 0.0 copy-start.5
  1.3 0.0 copy-start.4
  1.3 0.0 copy-start.8
  1.3 0.0 copy-start.9
  1.4 0.0 copy-done.10
  1.4 0.0 copy-done.11
  1.4 0.6 copy-done.5
  2.0 0.0 copy-done.4
  2.0 0.0 copy-done.8
  2.0 0.0 copy-done.9
  2.0 0.0 copy-start
  2.0 0.9 %copy-done = f32[3,4,16,128]{3,2,1,0:T(8,128)S(1)} copy-done((f32[3,4,16,128]{3,2,1,0:T(8,128)S(1)}, f32[3,4,16,128]{3,2,1,0:T(8,128)}, u32[]{:S(2)}) %copy-start) | copy-done | bytes 98328
  2.9 0.0 copy-start.1
  2.9 0.9 %copy-done.1 = f32[3,4,16,128]{3,2,1,0:T(8,128)S(1)} copy-done((f32[3,4,16,128]{3,2,1,0:T(8,128)S(1)}, f32[3,4,16,128]{3,2,1,0:T(8,128)}, u32[]{:S(2)}) %copy-start.1) | copy-done | bytes 98328
  3.8 0.0 copy-start.2
  3.8 0.9 %copy-done.2 = f32[3,4,16,128]{3,2,1,0:T(8,128)S(1)} copy-done((f32[3,4,16,128]{3,2,1,0:T(8,128)S(1)}, f32[3,4,16,128]{3,2,1,0:T(8,128)}, u32[]{:S(2)}) %copy-start.2) | copy-done | bytes 98328
  4.7 0.0 copy-start.3
  4.7 0.8 %copy-done.3 = s32[4,16,128]{2,1,0:T(8,128)S(1)} copy-done((s32[4,16,128]{2,1,0:T(8,128)S(1)}, s32[4,16,128]{2,1,0:T(8,128)}, u32[]{:S(2)}) %copy-start.3) | copy-done | bytes 32792
  5.5 0.0 copy-start.6
  5.5 0.7 copy-done.6
  6.2 0.0 copy-start.7
  6.2 0.7 copy-done.7
  6.8 60.7 %shard_map.148 = (f32[3,4,16,128]{3,2,1,0:T(8,128)S(1)}, f32[3,4,16,128]{3,2,1,0:T(8,128)S(1)}, f32[3,128]{1,0:T(4,128)S(1)}) custom-call(f32[3,4,16,128]{3,2,1,0:T(8,128)S(1)} %copy-done, f32[3,4,16,128]{3,2,1,0:T(8,128)S(1)} %copy-done.1, f32[3,4,16,128]{3,2,1,0:T(8,128)S(1)} %copy-done.2, s32[4,16,128]{2,1,0:T(8,128)S(1)} %copy-done.3, ...), custom_call_target="tpu_custom_call" | custom-call | tf_op jit(solution)/shard_map/pallas_call | solution.py:473
  67.5 0.6 copy.20
  68.2 0.6 copy.21
  68.8 0.6 copy.22
Async XLA Ops:
  0.6 0.7 %copy-start.10 = (f32[3]{0:T(128)S(1)}, f32[3]{0:T(128)}, u32[]{:S(2)}) copy-start(f32[3]{0:T(128)} %pla_ref.1) | copy-start | bytes 40
  0.6 0.7 %copy-start.11 = (f32[4]{0:T(128)S(1)}, f32[4]{0:T(128)}, u32[]{:S(2)}) copy-start(f32[4]{0:T(128)} %g_ref.1) | copy-start | bytes 52
  1.3 0.7 copy-start.5
  1.3 0.7 copy-start.4
  1.3 0.7 copy-start.8
  1.3 0.7 copy-start.9
  2.0 0.9 %copy-start = (f32[3,4,16,128]{3,2,1,0:T(8,128)S(1)}, f32[3,4,16,128]{3,2,1,0:T(8,128)}, u32[]{:S(2)}) copy-start(f32[3,4,16,128]{3,2,1,0:T(8,128)} %e_in.1) | copy-start | bytes 294916
  2.9 0.9 %copy-start.1 = (f32[3,4,16,128]{3,2,1,0:T(8,128)S(1)}, f32[3,4,16,128]{3,2,1,0:T(8,128)}, u32[]{:S(2)}) copy-start(f32[3,4,16,128]{3,2,1,0:T(8,128)} %h_in.1) | copy-start | bytes 294916
  3.8 0.9 %copy-start.2 = (f32[3,4,16,128]{3,2,1,0:T(8,128)S(1)}, f32[3,4,16,128]{3,2,1,0:T(8,128)}, u32[]{:S(2)}) copy-start(f32[3,4,16,128]{3,2,1,0:T(8,128)} %j_in.1) | copy-start | bytes 294916
  4.7 0.8 %copy-start.3 = (s32[4,16,128]{2,1,0:T(8,128)S(1)}, s32[4,16,128]{2,1,0:T(8,128)}, u32[]{:S(2)}) copy-start(s32[4,16,128]{2,1,0:T(8,128)} %mat_in.1) | copy-start | bytes 98308
  5.5 0.7 copy-start.6
  6.2 0.7 copy-start.7

commit v2 on v1

--- a/solution.py
+++ b/solution.py
@@ -18,7 +18,9 @@
 SLOTS = 1024
 TILE_DEV = 128
 NGX, NGY, NGZ = 16, 8, 4
-LANES = 16 * NGX
+NY_CHIPS, NZ_HI, NZ_LO, CORES = 4, 4, 4, 2
+NNEAR, NFAR = NY_CHIPS * CORES, NZ_HI * NZ_LO
+LANES = 16 * NFAR
 
 (XE, XQ, YE, YQ, ZE, ZQ, E_XZ, E_XY, E_YZ, E_YX, E_ZY, E_ZX) = range(12)
 ROUTES = (
@@ -55,6 +57,23 @@
     h_in,
     j_in,
     mat_in,
+    cell_in,
+    owner_in,
+    tile_in,
+    normal_in,
+    sig_in,
+    gam_in,
+    pla_in,
+    g_in,
+    count_ref,
+    e_out,
+    h_out,
+    force_out,
+    e_ref,
+    h_ref,
+    j_ref,
+    part,
+    mat_ref,
     cell_ref,
     owner_ref,
     tile_ref,
@@ -63,15 +82,7 @@
     gam_ref,
     pla_ref,
     g_ref,
-    count_ref,
-    e_out,
-    h_out,
     force_ref,
-    e_ref,
-    h_ref,
-    j_ref,
-    part,
-    mat_ref,
     coef,
     tensor,
     sx,
@@ -106,7 +117,22 @@
 
     loads = [
         pltpu.make_async_copy(src, dst, in_sem.at[n])
-        for n, (src, dst) in enumerate(((e_in, e_ref), (h_in, h_ref), (j_in, j_ref), (mat_in, mat_ref)))
+        for n, (src, dst) in enumerate(
+            (
+                (e_in, e_ref),
+                (h_in, h_ref),
+                (j_in, j_ref),
+                (mat_in, mat_ref),
+                (sig_in, sig_ref),
+                (gam_in, gam_ref),
+                (pla_in, pla_ref),
+                (g_in, g_ref),
+                (cell_in, cell_ref),
+                (owner_in, owner_ref),
+                (tile_in, tile_ref),
+                (normal_in, normal_ref),
+            )
+        )
     ]
     for load in loads:
         load.start()
@@ -116,17 +142,57 @@
         if dx:
             where["gx"] = lax.rem(gx + (dx + NGX), NGX)
         if dy:
-            where["gy"] = lax.rem(gy + (dy + NGY), NGY)
+            where["gy"] = gy + dy
         if dz:
             where["gz"] = lax.rem(gz + (dz + NGZ), NGZ)
         return where
 
+    y_chip, z_hi = lax.div(gx, NZ_HI), lax.rem(gx, NZ_HI)
+    z_lo, core = lax.div(gy, CORES), lax.rem(gy, CORES)
+    near, far = y_chip * CORES + core, z_hi * NZ_LO + z_lo
+
+    def near_at(n):
+        return {"gx": lax.div(n, CORES) * NZ_HI + z_hi, "gy": z_lo * CORES + lax.rem(n, CORES)}
+
+    def far_at(n):
+        return {"gx": y_chip * NZ_HI + lax.div(n, NZ_LO), "gy": lax.rem(n, NZ_LO) * CORES + core}
+
+    def sent(dy):
+        return gy > 0 if dy < 0 else gy < NGY - 1
+
+    def when(dy, do):
+        if dy:
+            pl.when(sent(dy))(do)
+        else:
+            do()
+
+    @pl.when(gy == NGY - 1)
+    def _():
+        for step in range(STEPS):
+            ry[step, 0:2] = jnp.zeros((2, CX, 1, CZ), F32)
+            ry[step, 5] = jnp.zeros((CX, 1, CZ), F32)
+            rr[step, 1] = jnp.zeros((1, CZ), F32)
+
+    @pl.when(gy == 0)
+    def _():
+        for step in range(STEPS):
+            ry[step, 2:5] = jnp.zeros((3, CX, 1, CZ), F32)
+            rr[step, 2] = jnp.zeros((1, CZ), F32)
+
     barrier = pltpu.get_barrier_semaphore()
-    greeted = list(ROUTES)
-    greeted += [(0, d, 0) for d in range(2, NGY - 1)]
-    greeted += [(d, 0, 0) for d in range(2, NGX - 1)]
-    for route in greeted:
-        pl.semaphore_signal(barrier, inc=1, device_id=at(*route), device_id_type=MESH)
+
+    def greet(where):
+        pl.semaphore_signal(barrier, inc=1, device_id=where, device_id_type=MESH)
+
+    for route in ROUTES:
+        when(route[1], functools.partial(lambda r: greet(at(*r)), route))
+    for d in range(1, NNEAR):
+        greet(near_at(lax.rem(near + d, NNEAR)))
+    for d in range(1, NFAR):
+        greet(far_at(lax.rem(far + d, NFAR)))
+    greeted = sum(route[1] == 0 for route in ROUTES) + NNEAR - 1 + NFAR - 1
+    greeted = greeted + sum(route[1] < 0 for route in ROUTES) * jnp.where(gy > 0, 1, 0)
+    greeted = greeted + sum(route[1] > 0 for route in ROUTES) * jnp.where(gy < NGY - 1, 1, 0)
 
     one, zero = jnp.float32(1.0), jnp.float32(0.0)
     low_x = jnp.where(gx > 0, one, zero)
@@ -177,27 +243,15 @@
             device_id_type=MESH,
         )
 
-    def send_electric(step):
+    def start(step, *which):
+        for n in which:
+            when(ROUTES[n][1], lambda n=n: message(step, n).start())
+
+    def send(step):
         ex, ey, ez = e_ref[0], e_ref[1], e_ref[2]
         sx[step, 0, 0] = ey[0]
         sx[step, 0, 1] = ez[0]
-        message(step, XE).start()
-        sr[step, 1] = ex[CX - 1, 0:1, :]
-        sr[step, 2] = ey[0, CY - 1 : CY, :]
-        sr[step, 0] = jnp.sum(ex[CX - 1, :, 0:1] * row_hot, axis=0, keepdims=True)
-        sr[step, 3] = jnp.sum(ez[0, :, CZ - 1 : CZ] * row_hot, axis=0, keepdims=True)
-        for which in (E_XY, E_YX, E_XZ, E_ZX):
-            message(step, which).start()
-        sy[step, 0] = ex[:, 0:1, :]
-        sy[step, 1] = ez[:, 0:1, :]
-        sy[step, 4] = ey[:, CY - 1 : CY, :]
-        sy[step, 5] = ez[:, 0:1, :]
-        sz[step, 0] = packed(e_ref[0:2][:, :, :, 0:1])
-        for which in (YE, ZE, E_YZ, E_ZY):
-            message(step, which).start()
-
-    def send_magnetic(step):
-        ex, ey, ez = e_ref[0], e_ref[1], e_ref[2]
+        start(step, XE)
         nothing = jnp.zeros((1, CY, CZ), F32)
         last_y, last_z = jj == CY - 1, kk == CZ - 1
         y_ez = jnp.where(last_y, zero, y_next(ez))
@@ -206,24 +260,34 @@
         z_ex = jnp.where(last_z, zero, z_next(ex))
         x_ez = jnp.concatenate([ez[1:], nothing], 0)
         x_ey = jnp.concatenate([ey[1:], nothing], 0)
-        hx = h_ref[0] - DT * ((y_ez - ez) - (z_ey - ey))
         hy = h_ref[1] - DT * ((z_ex - ex) - (x_ez - ez))
         hz = h_ref[2] - DT * ((x_ey - ey) - (y_ex - ex))
         sx[step, 1, 0] = hy[CX - 1]
         sx[step, 1, 1] = hz[CX - 1]
-        message(step, XQ).start()
+        start(step, XQ)
+        sr[step, 0] = jnp.sum(ex[CX - 1, :, 0:1] * row_hot, axis=0, keepdims=True)
+        sr[step, 1] = ex[CX - 1, 0:1, :]
+        sr[step, 2] = ey[0, CY - 1 : CY, :]
+        sr[step, 3] = jnp.sum(ez[0, :, CZ - 1 : CZ] * row_hot, axis=0, keepdims=True)
+        start(step, E_XZ, E_ZX, E_XY, E_YX)
+        hx = h_ref[0] - DT * ((y_ez - ez) - (z_ey - ey))
         part[0], part[1], part[2] = hx, hy, hz
+        sy[step, 0] = ex[:, 0:1, :]
+        sy[step, 1] = ez[:, 0:1, :]
         sy[step, 2] = hx[:, CY - 1 : CY, :]
         sy[step, 3] = hz[:, CY - 1 : CY, :]
+        sy[step, 4] = ey[:, CY - 1 : CY, :]
+        sy[step, 5] = ez[:, 0:1, :]
+        start(step, YE, YQ, E_YZ, E_ZY)
+        sz[step, 0] = packed(e_ref[0:2][:, :, :, 0:1])
         sz[step, 1] = packed(part[0:2][:, :, :, CZ - 1 : CZ])
-        message(step, YQ).start()
-        message(step, ZQ).start()
+        start(step, ZE, ZQ)
+
+    def update(step):
         j_ref[...] = coef[2][None] * j_ref[...] + coef[3][None] * e_ref[...]
-
-    def update(step):
         ex, ey, ez = e_ref[0], e_ref[1], e_ref[2]
         for which in range(12):
-            message(step, which).wait_recv()
+            when(-ROUTES[which][1], lambda which=which: message(step, which).wait_recv())
         above_x = rx[step, 0] * top_x
         above_y = ry[step, 0:2] * top_y
         above_z = unpacked(rz[step, 0]) * top_z
@@ -283,7 +347,7 @@
         earlier = (iota((block, block), 0) < iota((block, block), 1)).astype(F32).astype(BF16)
         lane = iota((1, block), 1)
         before = jnp.zeros((groups, 1), F32)
-        made = jnp.zeros((5 * NGY, LANES), F32)
+        made = jnp.zeros((5 * NNEAR, LANES), F32)
         for b in range(4):
             cut = slice(b * block, (b + 1) * block)
             own = owner[:, cut]
@@ -291,12 +355,12 @@
             ahead = dot(hot.astype(BF16), earlier, (1, 0)) + before
             rank = jnp.sum(ahead * hot, axis=0, keepdims=True).astype(jnp.int32)
             before = before + jnp.sum(hot, axis=1, keepdims=True)
-            place = rank * NGX + lax.shift_right_logical(own, 3)
+            place = rank * NFAR + (lax.shift_right_logical(own, 1) & (NFAR - 1))
             place_hot = (place == iota((LANES, block), 0)).astype(F32).astype(BF16)
             cell, normal = cell_ref[:, cut], normal_ref[:, cut]
-            live = (lane + b * block < count_ref[0]).astype(F32)
+            live = (lane + b * block < count_ref[0, 0, 0]).astype(F32)
             weight = live * (FACE_AREA * (1 - 2 * (normal & 1)).astype(F32))
-            mine = (own & 7) == iota((NGY, block), 0)
+            mine = lax.shift_right_logical(own, 5) * CORES + (own & 1) == iota((NNEAR, block), 0)
             entries = (
                 (cell & 127).astype(F32),
                 lax.shift_right_logical(cell, 7).astype(F32),
@@ -307,65 +371,70 @@
             rows = jnp.concatenate([jnp.where(mine, entry, zero) for entry in entries], 0)
             made = made + dot(rows.astype(BF16), place_hot, (1, 1))
         for n in range(5):
-            bucket[n] = made[n * NGY : (n + 1) * NGY].reshape(NGY, 1, LANES)
+            bucket[n] = made[n * NNEAR : (n + 1) * NNEAR].reshape(NNEAR, 1, LANES)
         stl[...] = bucket[4]
 
-    def to_gy(src, dst, send, recv, d):
+    def to_near(src, dst, send, recv, d):
+        n = lax.rem(near + d, NNEAR)
         return pltpu.make_async_remote_copy(
-            src_ref=src.at[lax.rem(gy + d, NGY)],
-            dst_ref=dst.at[gy],
+            src_ref=src.at[n],
+            dst_ref=dst.at[near],
             send_sem=send.at[d],
             recv_sem=recv.at[d],
-            device_id={"gy": lax.rem(gy + d, NGY)},
+            device_id=near_at(n),
             device_id_type=MESH,
         )
 
-    def from_gy(src, dst, send, recv, d):
+    def from_near(src, dst, send, recv, d):
+        n = lax.rem(near + NNEAR - d, NNEAR)
         return pltpu.make_async_remote_copy(
-            src_ref=src.at[lax.rem(gy + d, NGY)],
-            dst_ref=dst.at[lax.rem(gy + NGY - d, NGY)],
+            src_ref=src.at[n],
+            dst_ref=dst.at[n],
             send_sem=send.at[d],
             recv_sem=recv.at[d],
-            device_id={"gy": lax.rem(gy + d, NGY)},
+            device_id=near_at(n),
             device_id_type=MESH,
         )
 
     def lane_hots():
-        for n in range(NGY):
+        for n in range(NNEAR):
             lane_hot[n] = (bucket[0, n] == iota((CZ, LANES), 0).astype(F32)).astype(F32).astype(BF16)
 
     def tile_hots():
-        for d in range(1, NGY):
-            from_gy(stl, rtl, ts_sem, tr_sem, d).wait_recv()
-        for n in range(NGY):
+        for d in range(1, NNEAR):
+            from_near(stl, rtl, ts_sem, tr_sem, d).wait_recv()
+        for n in range(NNEAR):
             tile_hot[n] = (rtl[n] == iota((TILE_DEV, LANES), 0).astype(F32)).astype(F32).astype(BF16)
 
-    for load in loads:
-        load.wait()
-    material = mat_ref[...]
-
-    def of_material(table):
-        result = jnp.where(material == 0, table[0], zero)
-        for which in (1, 2):
-            result = jnp.where(material == which, table[which], result)
-        return result
-
-    sigma, gamma, plasma = of_material(sig_ref), of_material(gam_ref), of_material(pla_ref)
-    coef[0] = (1.0 - sigma * DT / 2) / (1.0 + sigma * DT / 2)
-    coef[1] = DT / (1.0 + sigma * DT / 2)
-    coef[2] = (1.0 - gamma * DT / 2) / (1.0 + gamma * DT / 2)
-    coef[3] = plasma * DT / (1.0 + gamma * DT / 2)
-
-    pl.semaphore_wait(barrier, len(greeted))
+    def coefficients():
+        material = mat_ref[...]
+
+        def of_material(table):
+            result = jnp.where(material == 0, table[0], zero)
+            for which in (1, 2):
+                result = jnp.where(material == which, table[which], result)
+            return result
+
+        sigma, gamma, plasma = of_material(sig_ref), of_material(gam_ref), of_material(pla_ref)
+        coef[0] = (1.0 - sigma * DT / 2) / (1.0 + sigma * DT / 2)
+        coef[1] = DT / (1.0 + sigma * DT / 2)
+        coef[2] = (1.0 - gamma * DT / 2) / (1.0 + gamma * DT / 2)
+        coef[3] = plasma * DT / (1.0 + gamma * DT / 2)
+
+    loads[0].wait()
+    loads[1].wait()
+    pl.semaphore_wait(barrier, greeted)
 
     for step in range(STEPS):
-        send_electric(step)
-        send_magnetic(step)
+        send(step)
         if step == 0:
+            for load in loads[2:]:
+                load.wait()
+            coefficients()
             ranks_and_buckets()
-            for d in range(1, NGY):
-                to_gy(stl, rtl, ts_sem, tr_sem, d).start()
-            rtl[gy] = stl[gy]
+            for d in range(1, NNEAR):
+                to_near(stl, rtl, ts_sem, tr_sem, d).start()
+            rtl[near] = stl[near]
         else:
             stress(step - 1)
         if step == 1:
@@ -383,7 +452,7 @@
     cells = CX * CY
     high, low = halves(tensor[...].reshape(6 * cells, CZ))
     parts = jnp.concatenate([high, low], 1)
-    for n in range(NGY):
+    for n in range(NNEAR):
         hot = lane_hot[n]
         read = dot(parts, jnp.concatenate([hot, hot], 0), (1, 0))
         row = bucket[1, n] == iota((cells, LANES), 0).astype(F32)
@@ -395,58 +464,74 @@
         sval[n, 0:1] = weight * jnp.where(along_x, xx, jnp.where(along_y, xy, xz))
         sval[n, 1:2] = weight * jnp.where(along_x, xy, jnp.where(along_y, yy, yz))
         sval[n, 2:3] = weight * jnp.where(along_x, xz, jnp.where(along_y, yz, zz))
-    for d in range(1, NGY):
-        to_gy(sval, rval, vs_sem, vr_sem, d).start()
-    rval[gy] = sval[gy]
-
-    for d in range(1, NGY):
-        from_gy(sval, rval, vs_sem, vr_sem, d).wait_recv()
-    row16 = iota((NGX * 16, LANES), 0)
-    mine = (lax.shift_right_logical(row16, 4) == (iota((NGX * 16, LANES), 1) & (NGX - 1))).astype(F32).astype(BF16)
-    dense = jnp.zeros((NGX * 16, TILE_DEV), F32)
-    for n in range(NGY):
+    for d in range(1, NNEAR):
+        to_near(sval, rval, vs_sem, vr_sem, d).start()
+    rval[near] = sval[near]
+
+    for d in range(1, NNEAR):
+        from_near(sval, rval, vs_sem, vr_sem, d).wait_recv()
+    row16 = iota((NFAR * 16, LANES), 0)
+    mine = (lax.shift_right_logical(row16, 4) == (iota((NFAR * 16, LANES), 1) & (NFAR - 1))).astype(F32).astype(BF16)
+    dense = jnp.zeros((NFAR * 16, TILE_DEV), F32)
+    for n in range(NNEAR):
         value = jnp.concatenate([rval[n], jnp.zeros((5, LANES), F32)], 0)
         high = value.astype(BF16).astype(F32)
         both = jnp.concatenate([high, value - high], 0).astype(BF16)
-        spread = jnp.concatenate([both] * NGX, 0) * mine
+        spread = jnp.concatenate([both] * NFAR, 0) * mine
         dense = dense + dot(spread, tile_hot[n], (1, 1))
-    dense = dense.reshape(NGX, 16, TILE_DEV)
+    dense = dense.reshape(NFAR, 16, TILE_DEV)
     sdense[...] = (dense[:, 0:8] + dense[:, 8:16])[:, 0:3]
 
-    def to_gx(d):
+    def to_far(d):
+        n = lax.rem(far + d, NFAR)
         return pltpu.make_async_remote_copy(
-            src_ref=sdense.at[lax.rem(gx + d, NGX)],
-            dst_ref=rdense.at[gx],
+            src_ref=sdense.at[n],
+            dst_ref=rdense.at[far],
             send_sem=ds_sem.at[d],
             recv_sem=dr_sem.at[d],
-            device_id={"gx": lax.rem(gx + d, NGX)},
+            device_id=far_at(n),
             device_id_type=MESH,
         )
 
-    for d in range(1, NGX):
-        to_gx(d).start()
-    rdense[gx] = sdense[gx]
-    for d in range(1, NGX):
-        pltpu.make_async_remote_copy(
-            src_ref=sdense.at[lax.rem(gx + d, NGX)],
-            dst_ref=rdense.at[lax.rem(gx + NGX - d, NGX)],
+    def from_far(d):
+        n = lax.rem(far + NFAR - d, NFAR)
+        return pltpu.make_async_remote_copy(
+            src_ref=sdense.at[n],
+            dst_ref=rdense.at[n],
             send_sem=ds_sem.at[d],
             recv_sem=dr_sem.at[d],
-            device_id={"gx": lax.rem(gx + d, NGX)},
+            device_id=far_at(n),
             device_id_type=MESH,
-        ).wait_recv()
+        )
+
+    for d in range(1, NFAR):
+        to_far(d).start()
+    rdense[far] = sdense[far]
+    for d in range(1, NFAR):
+        from_far(d).wait_recv()
     force_ref[...] = jnp.sum(rdense[...], axis=0)
 
     for step in range(STEPS):
         for which in range(12):
-            message(step, which).wait_send()
-    for d in range(1, NGY):
-        to_gy(stl, rtl, ts_sem, tr_sem, d).wait_send()
-        to_gy(sval, rval, vs_sem, vr_sem, d).wait_send()
-    for d in range(1, NGX):
-        to_gx(d).wait_send()
-    for store in stores:
+            when(ROUTES[which][1], lambda which=which: message(step, which).wait_send())
+    for d in range(1, NNEAR):
+        to_near(stl, rtl, ts_sem, tr_sem, d).wait_send()
+        to_near(sval, rval, vs_sem, vr_sem, d).wait_send()
+    for d in range(1, NFAR):
+        to_far(d).wait_send()
+    last = pltpu.make_async_copy(force_ref, force_out, out_sem.at[2])
+    last.start()
+    for store in [*stores, last]:
         store.wait()
+
+
+def hand_out(*refs):
+    sem = refs[-1]
+    copies = [pltpu.make_async_copy(refs[n], refs[n + 3], sem.at[n]) for n in range(3)]
+    for copy in copies:
+        copy.start()
+    for copy in copies:
+        copy.wait()
 
 
 def local(
@@ -465,22 +550,33 @@
     row_count,
 ):
     field = jax.ShapeDtypeStruct((3, CX, CY, CZ), F32)
-    hbm = pl.BlockSpec(memory_space=pl.ANY)
-    vmem = pl.BlockSpec(memory_space=pltpu.VMEM)
-    smem = pl.BlockSpec(memory_space=pltpu.SMEM)
+    hbm = pl.BlockSpec(memory_space=pltpu.HBM)
     dma = pltpu.SemaphoreType.DMA
     slots = [a.reshape(1, SLOTS) for a in (surf_cell, surf_owner, surf_tile, surf_normal)]
-    return pl.pallas_call(
+    operands = (e_field, h_field, current, material, *slots)
+    operands += (sigma_table, gamma_table, plasma_table, g_kernel)
+    operands = [pltpu.with_memory_space_constraint(a, pltpu.HBM) for a in operands]
+    shapes = (field, field, jax.ShapeDtypeStruct((3, TILE_DEV), F32))
+    made = pl.pallas_call(
         kernel,
-        out_shape=(field, field, jax.ShapeDtypeStruct((3, TILE_DEV), F32)),
-        in_specs=[hbm] * 4 + [vmem] * 4 + [smem] * 5,
-        out_specs=(hbm, hbm, vmem),
+        out_shape=shapes,
+        in_specs=[hbm] * 12 + [pl.BlockSpec(memory_space=pltpu.SMEM)],
+        out_specs=(hbm, hbm, hbm),
         scratch_shapes=[
             pltpu.VMEM((3, CX, CY, CZ), F32),
             pltpu.VMEM((3, CX, CY, CZ), F32),
             pltpu.VMEM((3, CX, CY, CZ), F32),
             pltpu.VMEM((3, CX, CY, CZ), F32),
             pltpu.VMEM((CX, CY, CZ), jnp.int32),
+            pltpu.VMEM((1, SLOTS), jnp.int32),
+            pltpu.VMEM((1, SLOTS), jnp.int32),
+            pltpu.VMEM((1, SLOTS), jnp.int32),
+            pltpu.VMEM((1, SLOTS), jnp.int32),
+            pltpu.SMEM((3,), F32),
+            pltpu.SMEM((3,), F32),
+            pltpu.SMEM((3,), F32),
+            pltpu.SMEM((STEPS,), F32),
+            pltpu.VMEM((3, TILE_DEV), F32),
             pltpu.VMEM((4, CX, CY, CZ), F32),
             pltpu.VMEM((6, CX, CY, CZ), F32),
             pltpu.VMEM((STEPS, 2, 2, CY, CZ), F32),
@@ -491,41 +587,38 @@
             pltpu.VMEM((STEPS, 2, 8, CZ), F32),
             pltpu.VMEM((STEPS, 4, 1, CZ), F32),
             pltpu.VMEM((STEPS, 4, 1, CZ), F32),
-            pltpu.VMEM((5, NGY, 1, LANES), F32),
-            pltpu.VMEM((NGY, CZ, LANES), BF16),
-            pltpu.VMEM((NGY, TILE_DEV, LANES), BF16),
-            pltpu.VMEM((NGY, 1, LANES), F32),
-            pltpu.VMEM((NGY, 1, LANES), F32),
-            pltpu.VMEM((NGY, 3, LANES), F32),
-            pltpu.VMEM((NGY, 3, LANES), F32),
-            pltpu.VMEM((NGX, 3, TILE_DEV), F32),
-            pltpu.VMEM((NGX, 3, TILE_DEV), F32),
-            dma((4,)),
-            dma((2,)),
+            pltpu.VMEM((5, NNEAR, 1, LANES), F32),
+            pltpu.VMEM((NNEAR, CZ, LANES), BF16),
+            pltpu.VMEM((NNEAR, TILE_DEV, LANES), BF16),
+            pltpu.VMEM((NNEAR, 1, LANES), F32),
+            pltpu.VMEM((NNEAR, 1, LANES), F32),
+            pltpu.VMEM((NNEAR, 3, LANES), F32),
+            pltpu.VMEM((NNEAR, 3, LANES), F32),
+            pltpu.VMEM((NFAR, 3, TILE_DEV), F32),
+            pltpu.VMEM((NFAR, 3, TILE_DEV), F32),
+            dma((12,)),
+            dma((3,)),
             dma((STEPS, 12)),
             dma((STEPS, 12)),
-            dma((NGY,)),
-            dma((NGY,)),
-            dma((NGY,)),
-            dma((NGY,)),
-            dma((NGX,)),
-            dma((NGX,)),
+            dma((NNEAR,)),
+            dma((NNEAR,)),
+            dma((NNEAR,)),
+            dma((NNEAR,)),
+            dma((NFAR,)),
+            dma((NFAR,)),
         ],
         compiler_params=pltpu.CompilerParams(
             collective_id=0, has_side_effects=True, vmem_limit_bytes=24 * 2**20
         ),
-    )(
-        e_field,
-        h_field,
-        current,
-        material,
-        *slots,
-        sigma_table,
-        gamma_table,
-        plasma_table,
-        g_kernel,
-        row_count.reshape(1),
-    )
+    )(*operands, row_count)
+    return pl.pallas_call(
+        hand_out,
+        out_shape=shapes,
+        in_specs=[hbm] * 3,
+        out_specs=(hbm,) * 3,
+        scratch_shapes=[dma((3,))],
+        compiler_params=pltpu.CompilerParams(vmem_limit_bytes=24 * 2**20),
+    )(*made)
 
 
 def solution(mesh):

time: 69.8 us -> 58.4 us (0.84)
  local copies, waits for them, and re-layouts: 7.33 us -> 0 us
  Pallas kernels: 60.7 us -> 57 us
    unnamed x27 -> x0, local copies, waits for them, and re-layouts: 7.33 us -> none
    pallas_call x1 -> x2, Pallas kernels: 60.7 us -> 57 us  [the longest x1 56.3 us: local(): pl.pallas_call(kernel, out_shape=shapes, in_specs=[hbm] * 12 + [pl.BlockS...]
where the time goes in v2:
time: 58.4 us; the launch traced here: 58.3 us
  Pallas kernels  57 us (98%)
  between operations  1.29 us (2%)
    pallas_call x1, Pallas kernels, local(): pl.pallas_call(kernel, out_shape=shapes, in_specs=[hbm] * 12 + [pl.BlockS...  56.3 us

profile of v2, /device:TPU:1, one launch (start us, length us, event | category | flops | bytes accessed | tf_op | source)
XLA Modules:
  0.0 58.3 jit_solution(1537268926341522883)
XLA Ops:
  1.3 56.3 %shard_map.148 = (f32[3,4,16,128]{3,2,1,0:T(8,128)S(1)}, f32[3,4,16,128]{3,2,1,0:T(8,128)S(1)}, f32[3,128]{1,0:T(4,128)S(1)}) custom-call(f32[3,4,16,128]{3,2,1,0:T(8,128)} %e_in.1, f32[3,4,16,128]{3,2,1,0:T(8,128)} %h_in.1, f32[3,4,16,128]{3,2,1,0:T(8,128)} %j_in.1, s32[4,16,128]{2,1,0:T(8,128)} %mat_in.1, s32[1,1024]{1,0:T(1,128)} %bitcast.4, ...), custom_call_target="tpu_custom_call" | custom-call | tf_op jit(solution)/shard_map/pallas_call | solution.py:560
  57.6 0.7 %shard_map.149 = (f32[3,4,16,128]{3,2,1,0:T(8,128)}, f32[3,4,16,128]{3,2,1,0:T(8,128)}, f32[3,128]{1,0:T(4,128)}) custom-call(f32[3,4,16,128]{3,2,1,0:T(8,128)S(1)} %get-tuple-element.6.refs_0_, f32[3,4,16,128]{3,2,1,0:T(8,128)S(1)} %get-tuple-element.7.refs_1_, f32[3,128]{1,0:T(4,128)S(1)} %get-tuple-element.8.refs_2_), custom_call_target="tpu_custom_call" | custom-call | tf_op jit(solution)/shard_map/pallas_call | solution.py:614

commit v3 on v2

--- a/solution.py
+++ b/solution.py
@@ -247,11 +247,26 @@
         for n in which:
             when(ROUTES[n][1], lambda n=n: message(step, n).start())
 
-    def send(step):
+    def send_x(step):
         ex, ey, ez = e_ref[0], e_ref[1], e_ref[2]
+        sr[step, 0] = jnp.sum(ex[CX - 1, :, 0:1] * row_hot, axis=0, keepdims=True)
+        sr[step, 3] = jnp.sum(ez[0, :, CZ - 1 : CZ] * row_hot, axis=0, keepdims=True)
+        start(step, E_XZ, E_ZX)
         sx[step, 0, 0] = ey[0]
         sx[step, 0, 1] = ez[0]
         start(step, XE)
+        ex, ey, ez = ex[CX - 1], ey[CX - 1], ez[CX - 1]
+        y_ex = jnp.where(jj[0] == CY - 1, zero, pltpu.roll(ex, CY - 1, 0))
+        z_ex = jnp.where(kk[0] == CZ - 1, zero, pltpu.roll(ex, CZ - 1, 1))
+        sx[step, 1, 0] = h_ref[1, CX - 1] - DT * ((z_ex - ex) + ez)
+        sx[step, 1, 1] = h_ref[2, CX - 1] + DT * (ey + (y_ex - ex))
+        start(step, XQ)
+        sr[step, 1] = ex[0:1, :]
+        sr[step, 2] = e_ref[1, 0, CY - 1 : CY, :]
+        start(step, E_XY, E_YX)
+
+    def send_yz(step):
+        ex, ey, ez = e_ref[0], e_ref[1], e_ref[2]
         nothing = jnp.zeros((1, CY, CZ), F32)
         last_y, last_z = jj == CY - 1, kk == CZ - 1
         y_ez = jnp.where(last_y, zero, y_next(ez))
@@ -260,18 +275,13 @@
         z_ex = jnp.where(last_z, zero, z_next(ex))
         x_ez = jnp.concatenate([ez[1:], nothing], 0)
         x_ey = jnp.concatenate([ey[1:], nothing], 0)
+        hx = h_ref[0] - DT * ((y_ez - ez) - (z_ey - ey))
         hy = h_ref[1] - DT * ((z_ex - ex) - (x_ez - ez))
         hz = h_ref[2] - DT * ((x_ey - ey) - (y_ex - ex))
-        sx[step, 1, 0] = hy[CX - 1]
-        sx[step, 1, 1] = hz[CX - 1]
-        start(step, XQ)
-        sr[step, 0] = jnp.sum(ex[CX - 1, :, 0:1] * row_hot, axis=0, keepdims=True)
-        sr[step, 1] = ex[CX - 1, 0:1, :]
-        sr[step, 2] = ey[0, CY - 1 : CY, :]
-        sr[step, 3] = jnp.sum(ez[0, :, CZ - 1 : CZ] * row_hot, axis=0, keepdims=True)
-        start(step, E_XZ, E_ZX, E_XY, E_YX)
-        hx = h_ref[0] - DT * ((y_ez - ez) - (z_ey - ey))
         part[0], part[1], part[2] = hx, hy, hz
+        sz[step, 0] = packed(e_ref[0:2][:, :, :, 0:1])
+        sz[step, 1] = packed(part[0:2][:, :, :, CZ - 1 : CZ])
+        start(step, ZE, ZQ)
         sy[step, 0] = ex[:, 0:1, :]
         sy[step, 1] = ez[:, 0:1, :]
         sy[step, 2] = hx[:, CY - 1 : CY, :]
@@ -279,56 +289,74 @@
         sy[step, 4] = ey[:, CY - 1 : CY, :]
         sy[step, 5] = ez[:, 0:1, :]
         start(step, YE, YQ, E_YZ, E_ZY)
-        sz[step, 0] = packed(e_ref[0:2][:, :, :, 0:1])
-        sz[step, 1] = packed(part[0:2][:, :, :, CZ - 1 : CZ])
-        start(step, ZE, ZQ)
+
+    def wait(step, *which):
+        for n in which:
+            when(-ROUTES[n][1], lambda n=n: message(step, n).wait_recv())
+
+    def current(step):
+        j_ref[...] = coef[2][None] * j_ref[...] + coef[3][None] * e_ref[...]
 
     def update(step):
-        j_ref[...] = coef[2][None] * j_ref[...] + coef[3][None] * e_ref[...]
+        last = CX - 1
+        wait(step, ZE, ZQ, YE, YQ, E_YZ, E_ZY)
         ex, ey, ez = e_ref[0], e_ref[1], e_ref[2]
-        for which in range(12):
-            when(-ROUTES[which][1], lambda which=which: message(step, which).wait_recv())
-        above_x = rx[step, 0] * top_x
-        above_y = ry[step, 0:2] * top_y
+        hx, hy, hz = part[0], part[1], part[2]
+        above_y = ry[step, 0:2]
         above_z = unpacked(rz[step, 0]) * top_z
-        hx, hy, hz = part[0], part[1], part[2]
         last_y, last_z = jj == CY - 1, kk == CZ - 1
         hx = hx + jnp.where(last_z, DT * above_z[1], zero) - jnp.where(last_y, DT * above_y[1], zero)
         hy = hy - jnp.where(last_z, DT * above_z[0], zero)
         hz = hz + jnp.where(last_y, DT * above_y[0], zero)
-        hy = jnp.concatenate([hy[: CX - 1], (hy[CX - 1] + DT * above_x[1])[None]], 0)
-        hz = jnp.concatenate([hz[: CX - 1], (hz[CX - 1] - DT * above_x[0])[None]], 0)
-        h_ref[0], h_ref[1], h_ref[2] = hx, hy, hz
-        e_xz = jnp.sum(rr[step, 0] * row_hot, axis=1, keepdims=True) * top_z
-        e_zx = jnp.sum(rr[step, 3] * row_hot, axis=1, keepdims=True) * top_x
-        e_xy = rr[step, 1] * top_y
-        e_yx = rr[step, 2] * top_x
         e_yz = ry[step, 4] * top_z
-        e_zy = ry[step, 5] * top_y
-        jr, kr = iota((CY, CZ), 0), iota((CY, CZ), 1)
-        below_xy = rx[step, 1, 0] + DT * ez[0] - jnp.where(kr == CZ - 1, DT * e_xz, zero)
-        below_xz = rx[step, 1, 1] - DT * ey[0] + jnp.where(jr == CY - 1, DT * e_xy, zero)
-        ky = iota((CX, 1, CZ), 2)
+        e_zy = ry[step, 5]
+        ky, jz = iota((CX, 1, CZ), 2), iota((CX, CY, 1), 1)
         below_yx = ry[step, 2] - DT * ez[:, 0:1, :] + jnp.where(ky == CZ - 1, DT * e_yz[:, :, 0:1], zero)
         below_yz = ry[step, 3] + DT * ex[:, 0:1, :]
-        below_yz = jnp.concatenate([below_yz[: CX - 1], (below_yz[CX - 1] - DT * e_yx)[None]], 0)
         below_z = unpacked(rz[step, 1])
-        jz = iota((CX, CY, 1), 1)
         below_zx = below_z[0] + DT * ey[:, :, 0:1] - jnp.where(jz == CY - 1, DT * e_zy[:, :, CZ - 1 : CZ], zero)
         below_zy = below_z[1] - DT * ex[:, :, 0:1]
-        below_zy = jnp.concatenate([below_zy[: CX - 1], (below_zy[CX - 1] + DT * e_zx)[None]], 0)
-
         first_y, first_z = jj == 0, kk == 0
         y_hx = jnp.where(first_y, low_y * below_yx, pltpu.roll(hx, 1, 1))
         y_hz = jnp.where(first_y, low_y * below_yz, pltpu.roll(hz, 1, 1))
         z_hx = jnp.where(first_z, low_z * below_zx, pltpu.roll(hx, 1, 2))
         z_hy = jnp.where(first_z, low_z * below_zy, pltpu.roll(hy, 1, 2))
-        x_hy = jnp.concatenate([(low_x * below_xy)[None], hy[: CX - 1]], 0)
-        x_hz = jnp.concatenate([(low_x * below_xz)[None], hz[: CX - 1]], 0)
+        nothing = jnp.zeros((1, CY, CZ), F32)
+        x_hy = jnp.concatenate([nothing, hy[:last]], 0)
+        x_hz = jnp.concatenate([nothing, hz[:last]], 0)
         keep, gain = coef[0], coef[1]
-        e_ref[0] = keep * ex + gain * (((hz - y_hz) - (hy - z_hy)) - j_ref[0])
-        e_ref[1] = keep * ey + gain * (((hx - z_hx) - (hz - x_hz)) - j_ref[1])
-        e_ref[2] = keep * ez + gain * (((hy - x_hy) - (hx - y_hx)) - j_ref[2])
+        part[0] = keep * ex + gain * (((hz - y_hz) - (hy - z_hy)) - j_ref[0])
+        part[1] = keep * ey + gain * (((hx - z_hx) - (hz - x_hz)) - j_ref[1])
+        part[2] = keep * ez + gain * (((hy - x_hy) - (hx - y_hx)) - j_ref[2])
+        h_ref[0], h_ref[1], h_ref[2] = hx, hy, hz
+
+        wait(step, E_XY, E_YX, XE, XQ)
+        jr, kr = jj[0], kk[0]
+        more_y = (DT * top_x) * rx[step, 0, 1]
+        more_z = (-DT * top_x) * rx[step, 0, 0]
+        e_yx = rr[step, 2] * top_x
+        h_ref[1, last] = h_ref[1, last] + more_y
+        h_ref[2, last] = h_ref[2, last] + more_z
+        y_more_z = jnp.where(jr == 0, (-DT * low_y) * e_yx, pltpu.roll(more_z, 1, 0))
+        z_more_y = jnp.where(kr == 0, zero, pltpu.roll(more_y, 1, 1))
+        gain = coef[1, last]
+        e_ref[0, 0:last] = part[0, 0:last]
+        e_ref[1, 1:last] = part[1, 1:last]
+        e_ref[2, 1:last] = part[2, 1:last]
+        x_last = part[0, last] + gain * ((more_z - y_more_z) - (more_y - z_more_y))
+        e_ref[1, last] = part[1, last] - gain * more_z
+        e_ref[2, last] = part[2, last] + gain * more_y
+        below_xy = rx[step, 1, 0] + DT * e_ref[2, 0]
+        below_xz = rx[step, 1, 1] - DT * e_ref[1, 0] + jnp.where(jr == CY - 1, DT * rr[step, 1], zero)
+        gain_0 = low_x * coef[1, 0]
+        z_first = part[2, 0] - gain_0 * below_xy
+        e_ref[1, 0] = part[1, 0] + gain_0 * below_xz
+
+        wait(step, E_XZ, E_ZX)
+        e_xz = jnp.sum(rr[step, 0] * row_hot, axis=1, keepdims=True) * (DT * top_z)
+        e_zx = jnp.sum(rr[step, 3] * row_hot, axis=1, keepdims=True) * (DT * top_x * low_z)
+        e_ref[2, 0] = z_first + jnp.where(kr == CZ - 1, gain_0 * e_xz, zero)
+        e_ref[0, last] = x_last + jnp.where(kr == 0, gain * e_zx, zero)
 
     def stress(step):
         ex, ey, ez = e_ref[0], e_ref[1], e_ref[2]
@@ -426,16 +454,19 @@
     pl.semaphore_wait(barrier, greeted)
 
     for step in range(STEPS):
-        send(step)
+        send_x(step)
+        send_yz(step)
         if step == 0:
             for load in loads[2:]:
                 load.wait()
             coefficients()
+            current(step)
             ranks_and_buckets()
             for d in range(1, NNEAR):
                 to_near(stl, rtl, ts_sem, tr_sem, d).start()
             rtl[near] = stl[near]
         else:
+            current(step)
             stress(step - 1)
         if step == 1:
             lane_hots()
@@ -470,17 +501,17 @@
 
     for d in range(1, NNEAR):
         from_near(sval, rval, vs_sem, vr_sem, d).wait_recv()
-    row16 = iota((NFAR * 16, LANES), 0)
-    mine = (lax.shift_right_logical(row16, 4) == (iota((NFAR * 16, LANES), 1) & (NFAR - 1))).astype(F32).astype(BF16)
-    dense = jnp.zeros((NFAR * 16, TILE_DEV), F32)
+    rows = (NFAR * 8, LANES)
+    mine = (lax.shift_right_logical(iota(rows, 0), 3) == (iota(rows, 1) & (NFAR - 1))).astype(F32)
+    dense = jnp.zeros((NFAR * 8, TILE_DEV), F32)
     for n in range(NNEAR):
-        value = jnp.concatenate([rval[n], jnp.zeros((5, LANES), F32)], 0)
+        value = rval[n]
         high = value.astype(BF16).astype(F32)
-        both = jnp.concatenate([high, value - high], 0).astype(BF16)
-        spread = jnp.concatenate([both] * NFAR, 0) * mine
+        both = jnp.concatenate([high, value - high, jnp.zeros((2, LANES), F32)], 0)
+        spread = (jnp.concatenate([both] * NFAR, 0) * mine).astype(BF16)
         dense = dense + dot(spread, tile_hot[n], (1, 1))
-    dense = dense.reshape(NFAR, 16, TILE_DEV)
-    sdense[...] = (dense[:, 0:8] + dense[:, 8:16])[:, 0:3]
+    dense = dense.reshape(NFAR, 8, TILE_DEV)
+    sdense[...] = dense[:, 0:3] + dense[:, 3:6]
 
     def to_far(d):
         n = lax.rem(far + d, NFAR)

time: 58.4 us -> 57.6 us (0.986)
  Pallas kernels: 57 us -> 56.2 us
    pallas_call x1, Pallas kernels: 56.3 us -> 55.5 us  [local(): pl.pallas_call(kernel, out_shape=shapes, in_specs=[hbm] * 12 + [pl.BlockS...]
where the time goes in v3:
time: 57.6 us; the launch traced here: 57.4 us
  Pallas kernels  56.2 us (98%)
  between operations  1.29 us (2%)
    pallas_call x1, Pallas kernels, local(): pl.pallas_call(kernel, out_shape=shapes, in_specs=[hbm] * 12 + [pl.BlockS...  55.5 us

profile of v3, /device:TPU:1, one launch (start us, length us, event | category | flops | bytes accessed | tf_op | source)
XLA Modules:
  0.0 57.4 jit_solution(17102946814488582726)
XLA Ops:
  1.3 55.5 %shard_map.148 = (f32[3,4,16,128]{3,2,1,0:T(8,128)S(1)}, f32[3,4,16,128]{3,2,1,0:T(8,128)S(1)}, f32[3,128]{1,0:T(4,128)S(1)}) custom-call(f32[3,4,16,128]{3,2,1,0:T(8,128)} %e_in.1, f32[3,4,16,128]{3,2,1,0:T(8,128)} %h_in.1, f32[3,4,16,128]{3,2,1,0:T(8,128)} %j_in.1, s32[4,16,128]{2,1,0:T(8,128)} %mat_in.1, s32[1,1024]{1,0:T(1,128)} %bitcast.4, ...), custom_call_target="tpu_custom_call" | custom-call | tf_op jit(solution)/shard_map/pallas_call | solution.py:591
  56.7 0.7 %shard_map.149 = (f32[3,4,16,128]{3,2,1,0:T(8,128)}, f32[3,4,16,128]{3,2,1,0:T(8,128)}, f32[3,128]{1,0:T(4,128)}) custom-call(f32[3,4,16,128]{3,2,1,0:T(8,128)S(1)} %get-tuple-element.6.refs_0_, f32[3,4,16,128]{3,2,1,0:T(8,128)S(1)} %get-tuple-element.7.refs_1_, f32[3,128]{1,0:T(4,128)S(1)} %get-tuple-element.8.refs_2_), custom_call_target="tpu_custom_call" | custom-call | tf_op jit(solution)/shard_map/pallas_call | solution.py:645

commit v4 on v3

--- a/solution.py
+++ b/solution.py
@@ -93,6 +93,9 @@
     rz,
     sr,
     rr,
+    sg,
+    rg,
+    rest,
     bucket,
     lane_hot,
     tile_hot,
@@ -112,6 +115,8 @@
     vr_sem,
     ds_sem,
     dr_sem,
+    gs_sem,
+    gr_sem,
 ):
     gx, gy, gz = lax.axis_index("gx"), lax.axis_index("gy"), lax.axis_index("gz")
 
@@ -205,6 +210,7 @@
     brick = (CX, CY, CZ)
     jj, kk = iota(brick, 1), iota(brick, 2)
     n_hot = (iota((16, 8, CZ), 0) == iota((16, 8, CZ), 2)).astype(F32)
+    n_more = (iota((2, 8, CZ), 0) + 16 == iota((2, 8, CZ), 2)).astype(F32)
     row_hot = (iota((CY, CZ), 0) == iota((CY, CZ), 1)).astype(F32)
 
     def y_next(f):
@@ -247,11 +253,31 @@
         for n in which:
             when(ROUTES[n][1], lambda n=n: message(step, n).start())
 
+    def as_row(column):
+        return jnp.sum(column * row_hot, axis=0, keepdims=True)
+
+    def as_column(row):
+        return jnp.sum(row * row_hot, axis=1, keepdims=True)
+
+    def send_edges(step, xz, zx):
+        sr[step, 0] = as_row(xz)
+        sr[step, 3] = as_row(zx)
+        start(step, E_XZ, E_ZX)
+
+    def edge_gain(n):
+        return pltpu.make_async_remote_copy(
+            src_ref=sg.at[n],
+            dst_ref=rg.at[n],
+            send_sem=gs_sem.at[n],
+            recv_sem=gr_sem.at[n],
+            device_id=at(*ROUTES[(E_XZ, E_ZX)[n]]),
+            device_id_type=MESH,
+        )
+
     def send_x(step):
         ex, ey, ez = e_ref[0], e_ref[1], e_ref[2]
-        sr[step, 0] = jnp.sum(ex[CX - 1, :, 0:1] * row_hot, axis=0, keepdims=True)
-        sr[step, 3] = jnp.sum(ez[0, :, CZ - 1 : CZ] * row_hot, axis=0, keepdims=True)
-        start(step, E_XZ, E_ZX)
+        if step == 0:
+            send_edges(0, ex[CX - 1, :, 0:1], ez[0, :, CZ - 1 : CZ])
         sx[step, 0, 0] = ey[0]
         sx[step, 0, 1] = ez[0]
         start(step, XE)
@@ -279,7 +305,7 @@
         hy = h_ref[1] - DT * ((z_ex - ex) - (x_ez - ez))
         hz = h_ref[2] - DT * ((x_ey - ey) - (y_ex - ex))
         part[0], part[1], part[2] = hx, hy, hz
-        sz[step, 0] = packed(e_ref[0:2][:, :, :, 0:1])
+        sz[step, 0] = packed(e_ref[0:2][:, :, :, 0:1]) + jnp.sum(ez[0].reshape(2, 8, CZ)[:, :, 0:1] * n_more, axis=0)
         sz[step, 1] = packed(part[0:2][:, :, :, CZ - 1 : CZ])
         start(step, ZE, ZQ)
         sy[step, 0] = ex[:, 0:1, :]
@@ -329,9 +355,36 @@
         part[1] = keep * ey + gain * (((hx - z_hx) - (hz - x_hz)) - j_ref[1])
         part[2] = keep * ez + gain * (((hy - x_hy) - (hx - y_hx)) - j_ref[2])
         h_ref[0], h_ref[1], h_ref[2] = hx, hy, hz
+        jr, kr = jj[0], kk[0]
+        if step < STEPS - 1:
+            send_edges(step + 1, part[0, last, :, 0:1], part[2, 0, :, CZ - 1 : CZ])
+
+        def edges():
+            wait(step, E_XZ, E_ZX)
+            e_xz, e_zx = as_column(rr[step, 0]), as_column(rr[step, 3])
+            if step == 1:
+                for n in range(2):
+                    edge_gain(n).wait_recv()
+            if step:
+                e_xz = e_xz + as_column(rg[0]) * rest[0]
+                e_zx = e_zx - as_column(rg[1]) * rest[1]
+            e_xz, e_zx = e_xz * (DT * top_z), e_zx * (DT * top_x)
+            if step < STEPS - 1:
+                more_z = jnp.broadcast_to(-DT * above_z[1, 0], (CY, CZ))
+                y_more_z = jnp.where(jr == 0, -DT * e_yz[0, :, 0:1], pltpu.roll(more_z, 1, 0))
+                more_y = DT * jnp.sum(rz[step, 0][None] * n_more, axis=2, keepdims=True).reshape(CY, 1)
+                rest[0] = (more_z - y_more_z) - (more_y - DT * ez[0, :, CZ - 1 : CZ])
+                rest[1] = jnp.broadcast_to(below_zy[last] + e_zx, (CY, CZ))
+            at_xz = jnp.where(kr == CZ - 1, low_x * coef[1, 0] * e_xz, zero)
+            at_zx = jnp.where(kr == 0, low_z * coef[1, last] * e_zx, zero)
+            return at_xz, at_zx
+
+        if step:
+            at_xz, at_zx = edges()
+            part[2, 0] = part[2, 0] + at_xz
+            part[0, last] = part[0, last] + at_zx
 
         wait(step, E_XY, E_YX, XE, XQ)
-        jr, kr = jj[0], kk[0]
         more_y = (DT * top_x) * rx[step, 0, 1]
         more_z = (-DT * top_x) * rx[step, 0, 0]
         e_yx = rr[step, 2] * top_x
@@ -352,11 +405,12 @@
         z_first = part[2, 0] - gain_0 * below_xy
         e_ref[1, 0] = part[1, 0] + gain_0 * below_xz
 
-        wait(step, E_XZ, E_ZX)
-        e_xz = jnp.sum(rr[step, 0] * row_hot, axis=1, keepdims=True) * (DT * top_z)
-        e_zx = jnp.sum(rr[step, 3] * row_hot, axis=1, keepdims=True) * (DT * top_x * low_z)
-        e_ref[2, 0] = z_first + jnp.where(kr == CZ - 1, gain_0 * e_xz, zero)
-        e_ref[0, last] = x_last + jnp.where(kr == 0, gain * e_zx, zero)
+        if step == 0:
+            at_xz, at_zx = edges()
+            z_first = z_first + at_xz
+            x_last = x_last + at_zx
+        e_ref[2, 0] = z_first
+        e_ref[0, last] = x_last
 
     def stress(step):
         ex, ey, ez = e_ref[0], e_ref[1], e_ref[2]
@@ -460,6 +514,10 @@
             for load in loads[2:]:
                 load.wait()
             coefficients()
+            sg[0] = as_row(coef[1, CX - 1, :, 0:1])
+            sg[1] = as_row(coef[1, 0, :, CZ - 1 : CZ])
+            for n in range(2):
+                edge_gain(n).start()
             current(step)
             ranks_and_buckets()
             for d in range(1, NNEAR):
@@ -545,6 +603,8 @@
     for step in range(STEPS):
         for which in range(12):
             when(ROUTES[which][1], lambda which=which: message(step, which).wait_send())
+    for n in range(2):
+        edge_gain(n).wait_send()
     for d in range(1, NNEAR):
         to_near(stl, rtl, ts_sem, tr_sem, d).wait_send()
         to_near(sval, rval, vs_sem, vr_sem, d).wait_send()
@@ -618,6 +678,9 @@
             pltpu.VMEM((STEPS, 2, 8, CZ), F32),
             pltpu.VMEM((STEPS, 4, 1, CZ), F32),
             pltpu.VMEM((STEPS, 4, 1, CZ), F32),
+            pltpu.VMEM((2, 1, CZ), F32),
+            pltpu.VMEM((2, 1, CZ), F32),
+            pltpu.VMEM((2, CY, CZ), F32),
             pltpu.VMEM((5, NNEAR, 1, LANES), F32),
             pltpu.VMEM((NNEAR, CZ, LANES), BF16),
             pltpu.VMEM((NNEAR, TILE_DEV, LANES), BF16),
@@ -637,6 +700,8 @@
             dma((NNEAR,)),
             dma((NFAR,)),
             dma((NFAR,)),
+            dma((2,)),
+            dma((2,)),
         ],
         compiler_params=pltpu.CompilerParams(
             collective_id=0, has_side_effects=True, vmem_limit_bytes=24 * 2**20

time: 57.6 us -> 55.5 us (0.964)
  Pallas kernels: 56.2 us -> 54.1 us
    pallas_call x1, Pallas kernels: 55.5 us -> 53.4 us  [local(): pl.pallas_call(kernel, out_shape=shapes, in_specs=[hbm] * 12 + [pl.BlockS...]
where the time goes in v4:
time: 55.5 us; the launch traced here: 55.3 us
  Pallas kernels  54.1 us (97%)
  between operations  1.29 us (2%)
    pallas_call x1, Pallas kernels, local(): pl.pallas_call(kernel, out_shape=shapes, in_specs=[hbm] * 12 + [pl.BlockS...  53.4 us

profile of v4, /device:TPU:1, one launch (start us, length us, event | category | flops | bytes accessed | tf_op | source)
XLA Modules:
  0.0 55.3 jit_solution(11536289985180050441)
XLA Ops:
  1.3 53.4 %shard_map.148 = (f32[3,4,16,128]{3,2,1,0:T(8,128)S(1)}, f32[3,4,16,128]{3,2,1,0:T(8,128)S(1)}, f32[3,128]{1,0:T(4,128)S(1)}) custom-call(f32[3,4,16,128]{3,2,1,0:T(8,128)} %e_in.1, f32[3,4,16,128]{3,2,1,0:T(8,128)} %h_in.1, f32[3,4,16,128]{3,2,1,0:T(8,128)} %j_in.1, s32[4,16,128]{2,1,0:T(8,128)} %mat_in.1, s32[1,1024]{1,0:T(1,128)} %bitcast.4, ...), custom_call_target="tpu_custom_call" | custom-call | tf_op jit(solution)/shard_map/pallas_call | solution.py:651
  54.6 0.7 %shard_map.149 = (f32[3,4,16,128]{3,2,1,0:T(8,128)}, f32[3,4,16,128]{3,2,1,0:T(8,128)}, f32[3,128]{1,0:T(4,128)}) custom-call(f32[3,4,16,128]{3,2,1,0:T(8,128)S(1)} %get-tuple-element.6.refs_0_, f32[3,4,16,128]{3,2,1,0:T(8,128)S(1)} %get-tuple-element.7.refs_1_, f32[3,128]{1,0:T(4,128)S(1)} %get-tuple-element.8.refs_2_), custom_call_target="tpu_custom_call" | custom-call | tf_op jit(solution)/shard_map/pallas_call | solution.py:710

commit v5 on v4

--- a/solution.py
+++ b/solution.py
@@ -68,7 +68,7 @@
     count_ref,
     e_out,
     h_out,
-    force_out,
+    force_ref,
     e_ref,
     h_ref,
     j_ref,
@@ -82,7 +82,6 @@
     gam_ref,
     pla_ref,
     g_ref,
-    force_ref,
     coef,
     tensor,
     sx,
@@ -139,7 +138,7 @@
             )
         )
     ]
-    for load in loads:
+    for load in loads[:2]:
         load.start()
 
     def at(dx, dy, dz):
@@ -171,6 +170,23 @@
         else:
             do()
 
+    barrier = pltpu.get_barrier_semaphore()
+
+    def greet(where):
+        pl.semaphore_signal(barrier, inc=1, device_id=where, device_id_type=MESH)
+
+    for d in range(1, NZ_LO):
+        greet({"gy": lax.rem(z_lo + d, NZ_LO) * CORES + core})
+    for route in sorted(ROUTES, key=lambda r: -abs(r[0])):
+        when(route[1], functools.partial(lambda r: greet(at(*r)), route))
+    for d in range(1, NNEAR):
+        greet(near_at(lax.rem(near + d, NNEAR)))
+    for load in loads[2:]:
+        load.start()
+    greeted = sum(route[1] == 0 for route in ROUTES) + NNEAR - 1 + NZ_LO - 1
+    greeted = greeted + sum(route[1] < 0 for route in ROUTES) * jnp.where(gy > 0, 1, 0)
+    greeted = greeted + sum(route[1] > 0 for route in ROUTES) * jnp.where(gy < NGY - 1, 1, 0)
+
     @pl.when(gy == NGY - 1)
     def _():
         for step in range(STEPS):
@@ -183,21 +199,6 @@
         for step in range(STEPS):
             ry[step, 2:5] = jnp.zeros((3, CX, 1, CZ), F32)
             rr[step, 2] = jnp.zeros((1, CZ), F32)
-
-    barrier = pltpu.get_barrier_semaphore()
-
-    def greet(where):
-        pl.semaphore_signal(barrier, inc=1, device_id=where, device_id_type=MESH)
-
-    for route in ROUTES:
-        when(route[1], functools.partial(lambda r: greet(at(*r)), route))
-    for d in range(1, NNEAR):
-        greet(near_at(lax.rem(near + d, NNEAR)))
-    for d in range(1, NFAR):
-        greet(far_at(lax.rem(far + d, NFAR)))
-    greeted = sum(route[1] == 0 for route in ROUTES) + NNEAR - 1 + NFAR - 1
-    greeted = greeted + sum(route[1] < 0 for route in ROUTES) * jnp.where(gy > 0, 1, 0)
-    greeted = greeted + sum(route[1] > 0 for route in ROUTES) * jnp.where(gy < NGY - 1, 1, 0)
 
     one, zero = jnp.float32(1.0), jnp.float32(0.0)
     low_x = jnp.where(gx > 0, one, zero)
@@ -274,22 +275,24 @@
             device_id_type=MESH,
         )
 
-    def send_x(step):
-        ex, ey, ez = e_ref[0], e_ref[1], e_ref[2]
-        if step == 0:
-            send_edges(0, ex[CX - 1, :, 0:1], ez[0, :, CZ - 1 : CZ])
-        sx[step, 0, 0] = ey[0]
-        sx[step, 0, 1] = ez[0]
-        start(step, XE)
-        ex, ey, ez = ex[CX - 1], ey[CX - 1], ez[CX - 1]
+    def send_sums(step, ex, ey, ez, hy, hz, y_first):
         y_ex = jnp.where(jj[0] == CY - 1, zero, pltpu.roll(ex, CY - 1, 0))
         z_ex = jnp.where(kk[0] == CZ - 1, zero, pltpu.roll(ex, CZ - 1, 1))
-        sx[step, 1, 0] = h_ref[1, CX - 1] - DT * ((z_ex - ex) + ez)
-        sx[step, 1, 1] = h_ref[2, CX - 1] + DT * (ey + (y_ex - ex))
+        sx[step, 1, 0] = hy - DT * ((z_ex - ex) + ez)
+        sx[step, 1, 1] = hz + DT * (ey + (y_ex - ex))
         start(step, XQ)
         sr[step, 1] = ex[0:1, :]
-        sr[step, 2] = e_ref[1, 0, CY - 1 : CY, :]
+        sr[step, 2] = y_first[CY - 1 : CY, :]
         start(step, E_XY, E_YX)
+
+    def send_x():
+        last = CX - 1
+        ey, ez = e_ref[1, 0], e_ref[2, 0]
+        send_edges(0, e_ref[0, last, :, 0:1], ez[:, CZ - 1 : CZ])
+        sx[0, 0, 0] = ey
+        sx[0, 0, 1] = ez
+        start(0, XE)
+        send_sums(0, e_ref[0, last], e_ref[1, last], e_ref[2, last], h_ref[1, last], h_ref[2, last], ey)
 
     def send_yz(step):
         ex, ey, ez = e_ref[0], e_ref[1], e_ref[2]
@@ -384,33 +387,40 @@
             part[2, 0] = part[2, 0] + at_xz
             part[0, last] = part[0, last] + at_zx
 
-        wait(step, E_XY, E_YX, XE, XQ)
+        gain_0 = low_x * coef[1, 0]
+        wait(step, E_XY, XQ)
+        below_xy = rx[step, 1, 0] + DT * ez[0]
+        below_xz = rx[step, 1, 1] - DT * ey[0] + jnp.where(jr == CY - 1, DT * rr[step, 1], zero)
+        y_first = part[1, 0] + gain_0 * below_xz
+        z_first = part[2, 0] - gain_0 * below_xy
+        if step == 0:
+            at_xz, at_zx = edges()
+            z_first = z_first + at_xz
+            part[0, last] = part[0, last] + at_zx
+        e_ref[1, 0], e_ref[2, 0] = y_first, z_first
+        if step < STEPS - 1:
+            sx[step + 1, 0, 0] = y_first
+            sx[step + 1, 0, 1] = z_first
+            start(step + 1, XE)
+        wait(step, E_YX, XE)
         more_y = (DT * top_x) * rx[step, 0, 1]
         more_z = (-DT * top_x) * rx[step, 0, 0]
         e_yx = rr[step, 2] * top_x
-        h_ref[1, last] = h_ref[1, last] + more_y
-        h_ref[2, last] = h_ref[2, last] + more_z
         y_more_z = jnp.where(jr == 0, (-DT * low_y) * e_yx, pltpu.roll(more_z, 1, 0))
         z_more_y = jnp.where(kr == 0, zero, pltpu.roll(more_y, 1, 1))
         gain = coef[1, last]
+        x_last = part[0, last] + gain * ((more_z - y_more_z) - (more_y - z_more_y))
+        y_last = part[1, last] - gain * more_z
+        z_last = part[2, last] + gain * more_y
+        hy_last = h_ref[1, last] + more_y
+        hz_last = h_ref[2, last] + more_z
+        h_ref[1, last], h_ref[2, last] = hy_last, hz_last
+        e_ref[0, last], e_ref[1, last], e_ref[2, last] = x_last, y_last, z_last
+        if step < STEPS - 1:
+            send_sums(step + 1, x_last, y_last, z_last, hy_last, hz_last, y_first)
         e_ref[0, 0:last] = part[0, 0:last]
         e_ref[1, 1:last] = part[1, 1:last]
         e_ref[2, 1:last] = part[2, 1:last]
-        x_last = part[0, last] + gain * ((more_z - y_more_z) - (more_y - z_more_y))
-        e_ref[1, last] = part[1, last] - gain * more_z
-        e_ref[2, last] = part[2, last] + gain * more_y
-        below_xy = rx[step, 1, 0] + DT * e_ref[2, 0]
-        below_xz = rx[step, 1, 1] - DT * e_ref[1, 0] + jnp.where(jr == CY - 1, DT * rr[step, 1], zero)
-        gain_0 = low_x * coef[1, 0]
-        z_first = part[2, 0] - gain_0 * below_xy
-        e_ref[1, 0] = part[1, 0] + gain_0 * below_xz
-
-        if step == 0:
-            at_xz, at_zx = edges()
-            z_first = z_first + at_xz
-            x_last = x_last + at_zx
-        e_ref[2, 0] = z_first
-        e_ref[0, last] = x_last
 
     def stress(step):
         ex, ey, ez = e_ref[0], e_ref[1], e_ref[2]
@@ -508,7 +518,8 @@
     pl.semaphore_wait(barrier, greeted)
 
     for step in range(STEPS):
-        send_x(step)
+        if step == 0:
+            send_x()
         send_yz(step)
         if step == 0:
             for load in loads[2:]:
@@ -593,13 +604,9 @@
             device_id_type=MESH,
         )
 
-    for d in range(1, NFAR):
+    for d in (8, 7, 9, 6, 10, 5, 11, 4, 12, 3, 13, 2, 14, 1, 15):
         to_far(d).start()
     rdense[far] = sdense[far]
-    for d in range(1, NFAR):
-        from_far(d).wait_recv()
-    force_ref[...] = jnp.sum(rdense[...], axis=0)
-
     for step in range(STEPS):
         for which in range(12):
             when(ROUTES[which][1], lambda which=which: message(step, which).wait_send())
@@ -610,10 +617,11 @@
         to_near(sval, rval, vs_sem, vr_sem, d).wait_send()
     for d in range(1, NFAR):
         to_far(d).wait_send()
-    last = pltpu.make_async_copy(force_ref, force_out, out_sem.at[2])
-    last.start()
-    for store in [*stores, last]:
+    for store in stores:
         store.wait()
+    for d in range(1, NFAR):
+        from_far(d).wait_recv()
+    force_ref[...] = jnp.sum(rdense[...], axis=0)
 
 
 def hand_out(*refs):
@@ -652,7 +660,7 @@
         kernel,
         out_shape=shapes,
         in_specs=[hbm] * 12 + [pl.BlockSpec(memory_space=pltpu.SMEM)],
-        out_specs=(hbm, hbm, hbm),
+        out_specs=(hbm, hbm, pl.BlockSpec(memory_space=pltpu.VMEM)),
         scratch_shapes=[
             pltpu.VMEM((3, CX, CY, CZ), F32),
             pltpu.VMEM((3, CX, CY, CZ), F32),
@@ -667,7 +675,6 @@
             pltpu.SMEM((3,), F32),
             pltpu.SMEM((3,), F32),
             pltpu.SMEM((STEPS,), F32),
-            pltpu.VMEM((3, TILE_DEV), F32),
             pltpu.VMEM((4, CX, CY, CZ), F32),
             pltpu.VMEM((6, CX, CY, CZ), F32),
             pltpu.VMEM((STEPS, 2, 2, CY, CZ), F32),
@@ -691,7 +698,7 @@
             pltpu.VMEM((NFAR, 3, TILE_DEV), F32),
             pltpu.VMEM((NFAR, 3, TILE_DEV), F32),
             dma((12,)),
-            dma((3,)),
+            dma((2,)),
             dma((STEPS, 12)),
             dma((STEPS, 12)),
             dma((NNEAR,)),

time: 55.5 us -> 53.3 us (0.960)
  Pallas kernels: 54.1 us -> 51.8 us
    pallas_call x1, Pallas kernels: 53.4 us -> 51.1 us  [local(): pl.pallas_call(kernel, out_shape=shapes, in_specs=[hbm] * 12 + [pl.BlockS...]
where the time goes in v5:
time: 53.3 us; the launch traced here: 53.1 us
  Pallas kernels  51.8 us (97%)
  between operations  1.29 us (2%)
    pallas_call x1, Pallas kernels, local(): pl.pallas_call(kernel, out_shape=shapes, in_specs=[hbm] * 12 + [pl.BlockS...  51.1 us

profile of v5, /device:TPU:1, one launch (start us, length us, event | category | flops | bytes accessed | tf_op | source)
XLA Modules:
  0.0 53.1 jit_solution(5254733324430414281)
XLA Ops:
  1.3 51.1 %shard_map.148 = (f32[3,4,16,128]{3,2,1,0:T(8,128)S(1)}, f32[3,4,16,128]{3,2,1,0:T(8,128)S(1)}, f32[3,128]{1,0:T(4,128)S(1)}) custom-call(f32[3,4,16,128]{3,2,1,0:T(8,128)} %e_in.1, f32[3,4,16,128]{3,2,1,0:T(8,128)} %h_in.1, f32[3,4,16,128]{3,2,1,0:T(8,128)} %j_in.1, s32[4,16,128]{2,1,0:T(8,128)} %mat_in.1, s32[1,1024]{1,0:T(1,128)} %bitcast.4, ...), custom_call_target="tpu_custom_call" | custom-call | tf_op jit(solution)/shard_map/pallas_call | solution.py:659
  52.4 0.7 %shard_map.149 = (f32[3,4,16,128]{3,2,1,0:T(8,128)}, f32[3,4,16,128]{3,2,1,0:T(8,128)}, f32[3,128]{1,0:T(4,128)}) custom-call(f32[3,4,16,128]{3,2,1,0:T(8,128)S(1)} %get-tuple-element.6.refs_0_, f32[3,4,16,128]{3,2,1,0:T(8,128)S(1)} %get-tuple-element.7.refs_1_, f32[3,128]{1,0:T(4,128)S(1)} %get-tuple-element.8.refs_2_), custom_call_target="tpu_custom_call" | custom-call | tf_op jit(solution)/shard_map/pallas_call | solution.py:717

commit v6 on v5

--- a/solution.py
+++ b/solution.py
@@ -144,7 +144,7 @@
     def at(dx, dy, dz):
         where = {}
         if dx:
-            where["gx"] = lax.rem(gx + (dx + NGX), NGX)
+            where["gx"] = gx + dx
         if dy:
             where["gy"] = gy + dy
         if dz:
@@ -161,12 +161,15 @@
     def far_at(n):
         return {"gx": y_chip * NZ_HI + lax.div(n, NZ_LO), "gy": lax.rem(n, NZ_LO) * CORES + core}
 
-    def sent(dy):
-        return gy > 0 if dy < 0 else gy < NGY - 1
-
-    def when(dy, do):
-        if dy:
-            pl.when(sent(dy))(do)
+    def inside(route, sign):
+        has = [gx < NGX - 1 if sign * route[0] > 0 else gx > 0] if route[0] else []
+        has += [gy < NGY - 1 if sign * route[1] > 0 else gy > 0] if route[1] else []
+        return has
+
+    def when(route, sign, do):
+        has = inside(route, sign)
+        if has:
+            pl.when(functools.reduce(jnp.logical_and, has))(do)
         else:
             do()
 
@@ -178,14 +181,33 @@
     for d in range(1, NZ_LO):
         greet({"gy": lax.rem(z_lo + d, NZ_LO) * CORES + core})
     for route in sorted(ROUTES, key=lambda r: -abs(r[0])):
-        when(route[1], functools.partial(lambda r: greet(at(*r)), route))
+        when(route, 1, functools.partial(lambda r: greet(at(*r)), route))
     for d in range(1, NNEAR):
         greet(near_at(lax.rem(near + d, NNEAR)))
     for load in loads[2:]:
         load.start()
-    greeted = sum(route[1] == 0 for route in ROUTES) + NNEAR - 1 + NZ_LO - 1
-    greeted = greeted + sum(route[1] < 0 for route in ROUTES) * jnp.where(gy > 0, 1, 0)
-    greeted = greeted + sum(route[1] > 0 for route in ROUTES) * jnp.where(gy < NGY - 1, 1, 0)
+    greeted = NNEAR - 1 + NZ_LO - 1
+    for route in ROUTES:
+        found = 1
+        for has in inside(route, 1):
+            found = found * jnp.where(has, 1, 0)
+        greeted = greeted + found
+
+    @pl.when(gx == NGX - 1)
+    def _():
+        for step in range(STEPS):
+            rx[step, 0] = jnp.zeros((2, CY, CZ), F32)
+            rr[step, 2] = jnp.zeros((1, CZ), F32)
+            rr[step, 3] = jnp.zeros((1, CZ), F32)
+        rg[1] = jnp.zeros((1, CZ), F32)
+
+    @pl.when(gx == 0)
+    def _():
+        for step in range(STEPS):
+            rx[step, 1] = jnp.zeros((2, CY, CZ), F32)
+            rr[step, 0] = jnp.zeros((1, CZ), F32)
+            rr[step, 1] = jnp.zeros((1, CZ), F32)
+        rg[0] = jnp.zeros((1, CZ), F32)
 
     @pl.when(gy == NGY - 1)
     def _():
@@ -252,7 +274,7 @@
 
     def start(step, *which):
         for n in which:
-            when(ROUTES[n][1], lambda n=n: message(step, n).start())
+            when(ROUTES[n], 1, lambda n=n: message(step, n).start())
 
     def as_row(column):
         return jnp.sum(column * row_hot, axis=0, keepdims=True)
@@ -275,15 +297,14 @@
             device_id_type=MESH,
         )
 
-    def send_sums(step, ex, ey, ez, hy, hz, y_first):
+    def send_sums(step, ex, ey, ez, hy, hz):
         y_ex = jnp.where(jj[0] == CY - 1, zero, pltpu.roll(ex, CY - 1, 0))
         z_ex = jnp.where(kk[0] == CZ - 1, zero, pltpu.roll(ex, CZ - 1, 1))
         sx[step, 1, 0] = hy - DT * ((z_ex - ex) + ez)
         sx[step, 1, 1] = hz + DT * (ey + (y_ex - ex))
         start(step, XQ)
         sr[step, 1] = ex[0:1, :]
-        sr[step, 2] = y_first[CY - 1 : CY, :]
-        start(step, E_XY, E_YX)
+        start(step, E_XY)
 
     def send_x():
         last = CX - 1
@@ -292,7 +313,9 @@
         sx[0, 0, 0] = ey
         sx[0, 0, 1] = ez
         start(0, XE)
-        send_sums(0, e_ref[0, last], e_ref[1, last], e_ref[2, last], h_ref[1, last], h_ref[2, last], ey)
+        send_sums(0, e_ref[0, last], e_ref[1, last], e_ref[2, last], h_ref[1, last], h_ref[2, last])
+        sr[0, 2] = ey[CY - 1 : CY, :]
+        start(0, E_YX)
 
     def send_yz(step):
         ex, ey, ez = e_ref[0], e_ref[1], e_ref[2]
@@ -321,7 +344,7 @@
 
     def wait(step, *which):
         for n in which:
-            when(-ROUTES[n][1], lambda n=n: message(step, n).wait_recv())
+            when(ROUTES[n], -1, lambda n=n: message(step, n).wait_recv())
 
     def current(step):
         j_ref[...] = coef[2][None] * j_ref[...] + coef[3][None] * e_ref[...]
@@ -367,7 +390,7 @@
             e_xz, e_zx = as_column(rr[step, 0]), as_column(rr[step, 3])
             if step == 1:
                 for n in range(2):
-                    edge_gain(n).wait_recv()
+                    when(ROUTES[(E_XZ, E_ZX)[n]], -1, edge_gain(n).wait_recv)
             if step:
                 e_xz = e_xz + as_column(rg[0]) * rest[0]
                 e_zx = e_zx - as_column(rg[1]) * rest[1]
@@ -387,37 +410,46 @@
             part[2, 0] = part[2, 0] + at_xz
             part[0, last] = part[0, last] + at_zx
 
-        gain_0 = low_x * coef[1, 0]
-        wait(step, E_XY, XQ)
-        below_xy = rx[step, 1, 0] + DT * ez[0]
-        below_xz = rx[step, 1, 1] - DT * ey[0] + jnp.where(jr == CY - 1, DT * rr[step, 1], zero)
-        y_first = part[1, 0] + gain_0 * below_xz
-        z_first = part[2, 0] - gain_0 * below_xy
+        later = step < STEPS - 1
+        gain_0, gain = low_x * coef[1, 0], coef[1, last]
         if step == 0:
             at_xz, at_zx = edges()
-            z_first = z_first + at_xz
+            part[2, 0] = part[2, 0] + at_xz
             part[0, last] = part[0, last] + at_zx
-        e_ref[1, 0], e_ref[2, 0] = y_first, z_first
-        if step < STEPS - 1:
-            sx[step + 1, 0, 0] = y_first
-            sx[step + 1, 0, 1] = z_first
-            start(step + 1, XE)
-        wait(step, E_YX, XE)
-        more_y = (DT * top_x) * rx[step, 0, 1]
-        more_z = (-DT * top_x) * rx[step, 0, 0]
-        e_yx = rr[step, 2] * top_x
-        y_more_z = jnp.where(jr == 0, (-DT * low_y) * e_yx, pltpu.roll(more_z, 1, 0))
-        z_more_y = jnp.where(kr == 0, zero, pltpu.roll(more_y, 1, 1))
-        gain = coef[1, last]
-        x_last = part[0, last] + gain * ((more_z - y_more_z) - (more_y - z_more_y))
-        y_last = part[1, last] - gain * more_z
-        z_last = part[2, last] + gain * more_y
-        hy_last = h_ref[1, last] + more_y
-        hz_last = h_ref[2, last] + more_z
-        h_ref[1, last], h_ref[2, last] = hy_last, hz_last
-        e_ref[0, last], e_ref[1, last], e_ref[2, last] = x_last, y_last, z_last
-        if step < STEPS - 1:
-            send_sums(step + 1, x_last, y_last, z_last, hy_last, hz_last, y_first)
+
+        def first_plane():
+            wait(step, E_XY, XQ)
+            below_xy = rx[step, 1, 0] + DT * ez[0]
+            below_xz = rx[step, 1, 1] - DT * ey[0] + jnp.where(jr == CY - 1, DT * rr[step, 1], zero)
+            y_first = part[1, 0] + gain_0 * below_xz
+            z_first = part[2, 0] - gain_0 * below_xy
+            if later:
+                sx[step + 1, 0, 0] = y_first
+                sx[step + 1, 0, 1] = z_first
+                start(step + 1, XE)
+                sr[step + 1, 2] = y_first[CY - 1 : CY, :]
+                start(step + 1, E_YX)
+            e_ref[1, 0], e_ref[2, 0] = y_first, z_first
+
+        def last_plane():
+            wait(step, E_YX, XE)
+            more_y = (DT * top_x) * rx[step, 0, 1]
+            more_z = (-DT * top_x) * rx[step, 0, 0]
+            e_yx = rr[step, 2] * top_x
+            y_more_z = jnp.where(jr == 0, (-DT * low_y) * e_yx, pltpu.roll(more_z, 1, 0))
+            z_more_y = jnp.where(kr == 0, zero, pltpu.roll(more_y, 1, 1))
+            x_last = part[0, last] + gain * ((more_z - y_more_z) - (more_y - z_more_y))
+            y_last = part[1, last] - gain * more_z
+            z_last = part[2, last] + gain * more_y
+            hy_last = h_ref[1, last] + more_y
+            hz_last = h_ref[2, last] + more_z
+            if later:
+                send_sums(step + 1, x_last, y_last, z_last, hy_last, hz_last)
+            h_ref[1, last], h_ref[2, last] = hy_last, hz_last
+            e_ref[0, last], e_ref[1, last], e_ref[2, last] = x_last, y_last, z_last
+
+        for plane in (first_plane, last_plane):
+            plane()
         e_ref[0, 0:last] = part[0, 0:last]
         e_ref[1, 1:last] = part[1, 1:last]
         e_ref[2, 1:last] = part[2, 1:last]
@@ -466,27 +498,38 @@
             bucket[n] = made[n * NNEAR : (n + 1) * NNEAR].reshape(NNEAR, 1, LANES)
         stl[...] = bucket[4]
 
-    def to_near(src, dst, send, recv, d):
-        n = lax.rem(near + d, NNEAR)
+    def toward(k):
+        return lax.rem(y_chip + k // CORES, NY_CHIPS) * CORES + lax.rem(core + k % CORES, CORES)
+
+    def origin(k):
+        return lax.rem(y_chip + NY_CHIPS - k // CORES, NY_CHIPS) * CORES + lax.rem(core + k % CORES, CORES)
+
+    def to_near(src, dst, send, recv, k):
         return pltpu.make_async_remote_copy(
-            src_ref=src.at[n],
+            src_ref=src,
             dst_ref=dst.at[near],
-            send_sem=send.at[d],
-            recv_sem=recv.at[d],
+            send_sem=send.at[k],
+            recv_sem=recv.at[k],
+            device_id=near_at(toward(k)),
+            device_id_type=MESH,
+        )
+
+    def from_near(dst, send, recv, k):
+        n = origin(k)
+        return pltpu.make_async_remote_copy(
+            src_ref=dst.at[n],
+            dst_ref=dst.at[n],
+            send_sem=send.at[k],
+            recv_sem=recv.at[k],
             device_id=near_at(n),
             device_id_type=MESH,
         )
 
-    def from_near(src, dst, send, recv, d):
-        n = lax.rem(near + NNEAR - d, NNEAR)
-        return pltpu.make_async_remote_copy(
-            src_ref=src.at[n],
-            dst_ref=dst.at[n],
-            send_sem=send.at[d],
-            recv_sem=recv.at[d],
-            device_id=near_at(n),
-            device_id_type=MESH,
-        )
+    def tiles_to(k):
+        return to_near(stl.at[toward(k)], rtl, ts_sem, tr_sem, k)
+
+    def values_to(k):
+        return to_near(sval.at[k], rval, vs_sem, vr_sem, k)
 
     def lane_hots():
         for n in range(NNEAR):
@@ -494,7 +537,7 @@
 
     def tile_hots():
         for d in range(1, NNEAR):
-            from_near(stl, rtl, ts_sem, tr_sem, d).wait_recv()
+            from_near(rtl, ts_sem, tr_sem, d).wait_recv()
         for n in range(NNEAR):
             tile_hot[n] = (rtl[n] == iota((TILE_DEV, LANES), 0).astype(F32)).astype(F32).astype(BF16)
 
@@ -528,11 +571,11 @@
             sg[0] = as_row(coef[1, CX - 1, :, 0:1])
             sg[1] = as_row(coef[1, 0, :, CZ - 1 : CZ])
             for n in range(2):
-                edge_gain(n).start()
+                when(ROUTES[(E_XZ, E_ZX)[n]], 1, edge_gain(n).start)
             current(step)
             ranks_and_buckets()
             for d in range(1, NNEAR):
-                to_near(stl, rtl, ts_sem, tr_sem, d).start()
+                tiles_to(d).start()
             rtl[near] = stl[near]
         else:
             current(step)
@@ -552,7 +595,8 @@
     cells = CX * CY
     high, low = halves(tensor[...].reshape(6 * cells, CZ))
     parts = jnp.concatenate([high, low], 1)
-    for n in range(NNEAR):
+    for k in (4, 5, 2, 3, 6, 7, 1, 0):
+        n = toward(k)
         hot = lane_hot[n]
         read = dot(parts, jnp.concatenate([hot, hot], 0), (1, 0))
         row = bucket[1, n] == iota((cells, LANES), 0).astype(F32)
@@ -561,19 +605,20 @@
         ]
         axis, weight = bucket[3, n], bucket[2, n]
         along_x, along_y = axis == 0.0, axis == 1.0
-        sval[n, 0:1] = weight * jnp.where(along_x, xx, jnp.where(along_y, xy, xz))
-        sval[n, 1:2] = weight * jnp.where(along_x, xy, jnp.where(along_y, yy, yz))
-        sval[n, 2:3] = weight * jnp.where(along_x, xz, jnp.where(along_y, yz, zz))
-    for d in range(1, NNEAR):
-        to_near(sval, rval, vs_sem, vr_sem, d).start()
-    rval[near] = sval[near]
-
-    for d in range(1, NNEAR):
-        from_near(sval, rval, vs_sem, vr_sem, d).wait_recv()
+        sval[k, 0:1] = weight * jnp.where(along_x, xx, jnp.where(along_y, xy, xz))
+        sval[k, 1:2] = weight * jnp.where(along_x, xy, jnp.where(along_y, yy, yz))
+        sval[k, 2:3] = weight * jnp.where(along_x, xz, jnp.where(along_y, yz, zz))
+        if k:
+            values_to(k).start()
+    rval[near] = sval[0]
+
     rows = (NFAR * 8, LANES)
     mine = (lax.shift_right_logical(iota(rows, 0), 3) == (iota(rows, 1) & (NFAR - 1))).astype(F32)
     dense = jnp.zeros((NFAR * 8, TILE_DEV), F32)
-    for n in range(NNEAR):
+    for k in (0, 1, 2, 3, 6, 7, 4, 5):
+        n = origin(k)
+        if k:
+            from_near(rval, vs_sem, vr_sem, k).wait_recv()
         value = rval[n]
         high = value.astype(BF16).astype(F32)
         both = jnp.concatenate([high, value - high, jnp.zeros((2, LANES), F32)], 0)
@@ -609,12 +654,12 @@
     rdense[far] = sdense[far]
     for step in range(STEPS):
         for which in range(12):
-            when(ROUTES[which][1], lambda which=which: message(step, which).wait_send())
+            when(ROUTES[which], 1, lambda which=which: message(step, which).wait_send())
     for n in range(2):
-        edge_gain(n).wait_send()
+        when(ROUTES[(E_XZ, E_ZX)[n]], 1, edge_gain(n).wait_send)
     for d in range(1, NNEAR):
-        to_near(stl, rtl, ts_sem, tr_sem, d).wait_send()
-        to_near(sval, rval, vs_sem, vr_sem, d).wait_send()
+        tiles_to(d).wait_send()
+        values_to(d).wait_send()
     for d in range(1, NFAR):
         to_far(d).wait_send()
     for store in stores:

time: 53.3 us -> 51.9 us (0.974)
  Pallas kernels: 51.8 us -> 50.5 us
    pallas_call x1, Pallas kernels: 51.1 us -> 49.8 us  [local(): pl.pallas_call(kernel, out_shape=shapes, in_specs=[hbm] * 12 + [pl.BlockS...]
where the time goes in v6:
time: 51.9 us; the launch traced here: 51.8 us
  Pallas kernels  50.5 us (97%)
  between operations  1.29 us (2%)
    pallas_call x1, Pallas kernels, local(): pl.pallas_call(kernel, out_shape=shapes, in_specs=[hbm] * 12 + [pl.BlockS...  49.8 us

profile of v6, /device:TPU:1, one launch (start us, length us, event | category | flops | bytes accessed | tf_op | source)
XLA Modules:
  0.0 51.8 jit_solution(4188148733304964062)
XLA Ops:
  1.3 49.8 %shard_map.148 = (f32[3,4,16,128]{3,2,1,0:T(8,128)S(1)}, f32[3,4,16,128]{3,2,1,0:T(8,128)S(1)}, f32[3,128]{1,0:T(4,128)S(1)}) custom-call(f32[3,4,16,128]{3,2,1,0:T(8,128)} %e_in.1, f32[3,4,16,128]{3,2,1,0:T(8,128)} %h_in.1, f32[3,4,16,128]{3,2,1,0:T(8,128)} %j_in.1, s32[4,16,128]{2,1,0:T(8,128)} %mat_in.1, s32[1,1024]{1,0:T(1,128)} %bitcast.4, ...), custom_call_target="tpu_custom_call" | custom-call | tf_op jit(solution)/shard_map/pallas_call | solution.py:704
  51.0 0.7 %shard_map.149 = (f32[3,4,16,128]{3,2,1,0:T(8,128)}, f32[3,4,16,128]{3,2,1,0:T(8,128)}, f32[3,128]{1,0:T(4,128)}) custom-call(f32[3,4,16,128]{3,2,1,0:T(8,128)S(1)} %get-tuple-element.6.refs_0_, f32[3,4,16,128]{3,2,1,0:T(8,128)S(1)} %get-tuple-element.7.refs_1_, f32[3,128]{1,0:T(4,128)S(1)} %get-tuple-element.8.refs_2_), custom_call_target="tpu_custom_call" | custom-call | tf_op jit(solution)/shard_map/pallas_call | solution.py:762

commit v7 on v6

--- a/solution.py
+++ b/solution.py
@@ -148,7 +148,7 @@
         if dy:
             where["gy"] = gy + dy
         if dz:
-            where["gz"] = lax.rem(gz + (dz + NGZ), NGZ)
+            where["gz"] = gz + dz
         return where
 
     y_chip, z_hi = lax.div(gx, NZ_HI), lax.rem(gx, NZ_HI)
@@ -164,6 +164,7 @@
     def inside(route, sign):
         has = [gx < NGX - 1 if sign * route[0] > 0 else gx > 0] if route[0] else []
         has += [gy < NGY - 1 if sign * route[1] > 0 else gy > 0] if route[1] else []
+        has += [gz < NGZ - 1 if sign * route[2] > 0 else gz > 0] if route[2] else []
         return has
 
     def when(route, sign, do):
@@ -192,6 +193,22 @@
         for has in inside(route, 1):
             found = found * jnp.where(has, 1, 0)
         greeted = greeted + found
+
+    @pl.when(gz == NGZ - 1)
+    def _():
+        for step in range(STEPS):
+            rz[step, 0] = jnp.zeros((8, CZ), F32)
+            ry[step, 4] = jnp.zeros((CX, 1, CZ), F32)
+            rr[step, 0] = jnp.zeros((1, CZ), F32)
+        rg[0] = jnp.zeros((1, CZ), F32)
+
+    @pl.when(gz == 0)
+    def _():
+        for step in range(STEPS):
+            rz[step, 1] = jnp.zeros((8, CZ), F32)
+            ry[step, 5] = jnp.zeros((CX, 1, CZ), F32)
+            rr[step, 3] = jnp.zeros((1, CZ), F32)
+        rg[1] = jnp.zeros((1, CZ), F32)
 
     @pl.when(gx == NGX - 1)
     def _():

time: 51.9 us -> 50.7 us (0.977)
  Pallas kernels: 50.5 us -> 49.2 us
    pallas_call x1, Pallas kernels: 49.8 us -> 48.5 us  [local(): pl.pallas_call(kernel, out_shape=shapes, in_specs=[hbm] * 12 + [pl.BlockS...]
where the time goes in v7:
time: 50.7 us; the launch traced here: 50.5 us
  Pallas kernels  49.2 us (97%)
  between operations  1.29 us (3%)
    pallas_call x1, Pallas kernels, local(): pl.pallas_call(kernel, out_shape=shapes, in_specs=[hbm] * 12 + [pl.BlockS...  48.5 us

profile of v7, /device:TPU:1, one launch (start us, length us, event | category | flops | bytes accessed | tf_op | source)
XLA Modules:
  0.0 50.5 jit_solution(12283684566208800136)
XLA Ops:
  1.3 48.5 %shard_map.148 = (f32[3,4,16,128]{3,2,1,0:T(8,128)S(1)}, f32[3,4,16,128]{3,2,1,0:T(8,128)S(1)}, f32[3,128]{1,0:T(4,128)S(1)}) custom-call(f32[3,4,16,128]{3,2,1,0:T(8,128)} %e_in.1, f32[3,4,16,128]{3,2,1,0:T(8,128)} %h_in.1, f32[3,4,16,128]{3,2,1,0:T(8,128)} %j_in.1, s32[4,16,128]{2,1,0:T(8,128)} %mat_in.1, s32[1,1024]{1,0:T(1,128)} %bitcast.4, ...), custom_call_target="tpu_custom_call" | custom-call | tf_op jit(solution)/shard_map/pallas_call | solution.py:721
  49.8 0.7 %shard_map.149 = (f32[3,4,16,128]{3,2,1,0:T(8,128)}, f32[3,4,16,128]{3,2,1,0:T(8,128)}, f32[3,128]{1,0:T(4,128)}) custom-call(f32[3,4,16,128]{3,2,1,0:T(8,128)S(1)} %get-tuple-element.6.refs_0_, f32[3,4,16,128]{3,2,1,0:T(8,128)S(1)} %get-tuple-element.7.refs_1_, f32[3,128]{1,0:T(4,128)S(1)} %get-tuple-element.8.refs_2_), custom_call_target="tpu_custom_call" | custom-call | tf_op jit(solution)/shard_map/pallas_call | solution.py:779

commit v8 on v7

--- a/solution.py
+++ b/solution.py
@@ -289,7 +289,12 @@
             device_id_type=MESH,
         )
 
+    entered, held = [], []
+
     def start(step, *which):
+        if not entered:
+            held.append((step, *which))
+            return
         for n in which:
             when(ROUTES[n], 1, lambda n=n: message(step, n).start())
 
@@ -465,7 +470,7 @@
             h_ref[1, last], h_ref[2, last] = hy_last, hz_last
             e_ref[0, last], e_ref[1, last], e_ref[2, last] = x_last, y_last, z_last
 
-        for plane in (first_plane, last_plane):
+        for plane in (last_plane, first_plane):
             plane()
         e_ref[0, 0:last] = part[0, 0:last]
         e_ref[1, 1:last] = part[1, 1:last]
@@ -575,12 +580,16 @@
 
     loads[0].wait()
     loads[1].wait()
+    send_x()
+    send_yz(0)
     pl.semaphore_wait(barrier, greeted)
+    entered.append(True)
+    for which in held:
+        start(*which)
 
     for step in range(STEPS):
-        if step == 0:
-            send_x()
-        send_yz(step)
+        if step:
+            send_yz(step)
         if step == 0:
             for load in loads[2:]:
                 load.wait()
@@ -590,16 +599,17 @@
             for n in range(2):
                 when(ROUTES[(E_XZ, E_ZX)[n]], 1, edge_gain(n).start)
             current(step)
+        else:
+            current(step)
+            stress(step - 1)
+        if step == 1:
             ranks_and_buckets()
             for d in range(1, NNEAR):
                 tiles_to(d).start()
             rtl[near] = stl[near]
-        else:
-            current(step)
-            stress(step - 1)
-        if step == 1:
+        if step == 2:
             lane_hots()
-        if step == 2:
+        if step == 3:
             tile_hots()
         update(step)
     stores = [

time: 50.7 us -> 50.5 us (level)
  no operation moved by 1% of the time
where the time goes in v8:
time: 50.5 us; the launch traced here: 50.2 us
  Pallas kernels  48.9 us (97%)
  between operations  1.29 us (3%)
    pallas_call x1, Pallas kernels, local(): pl.pallas_call(kernel, out_shape=shapes, in_specs=[hbm] * 12 + [pl.BlockS...  48.2 us

profile of v8, /device:TPU:1, one launch (start us, length us, event | category | flops | bytes accessed | tf_op | source)
XLA Modules:
  0.0 50.2 jit_solution(2735103117887030988)
XLA Ops:
  1.3 48.2 %shard_map.148 = (f32[3,4,16,128]{3,2,1,0:T(8,128)S(1)}, f32[3,4,16,128]{3,2,1,0:T(8,128)S(1)}, f32[3,128]{1,0:T(4,128)S(1)}) custom-call(f32[3,4,16,128]{3,2,1,0:T(8,128)} %e_in.1, f32[3,4,16,128]{3,2,1,0:T(8,128)} %h_in.1, f32[3,4,16,128]{3,2,1,0:T(8,128)} %j_in.1, s32[4,16,128]{2,1,0:T(8,128)} %mat_in.1, s32[1,1024]{1,0:T(1,128)} %bitcast.4, ...), custom_call_target="tpu_custom_call" | custom-call | tf_op jit(solution)/shard_map/pallas_call | solution.py:731
  49.5 0.7 %shard_map.149 = (f32[3,4,16,128]{3,2,1,0:T(8,128)}, f32[3,4,16,128]{3,2,1,0:T(8,128)}, f32[3,128]{1,0:T(4,128)}) custom-call(f32[3,4,16,128]{3,2,1,0:T(8,128)S(1)} %get-tuple-element.6.refs_0_, f32[3,4,16,128]{3,2,1,0:T(8,128)S(1)} %get-tuple-element.7.refs_1_, f32[3,128]{1,0:T(4,128)S(1)} %get-tuple-element.8.refs_2_), custom_call_target="tpu_custom_call" | custom-call | tf_op jit(solution)/shard_map/pallas_call | solution.py:789
